TPU v7x, 256 devices: a whole 4x4x8 slice. The times are simulated.
256 devices in a mesh: dp: 32 (over x, y, core), rep: 8 (over z).
Axes of the slice: x: 4, y: 4, z: 8, core: 2. Of those that a mesh axis runs over, the one named last changes fastest.
Arguments:
- residual_in: bfloat16 [2048, 3584], P(('rep', 'dp')), parts along dimension 0, may hold values from -3 to 3
- q_latent: bfloat16 [2048, 128, 512], P(('rep', 'dp')), parts along dimension 0
- q_rope: bfloat16 [2048, 64, 128], P(('rep', 'dp')), parts along dimension 0, may hold values from -6 to 6
- cache_latent: bfloat16 [2048, 384, 512], P(('rep', 'dp')), parts along dimension 0
- cache_rope: bfloat16 [2048, 64, 384], P(('rep', 'dp')), parts along dimension 0, may hold values from -6 to 6
- new_latent: bfloat16 [2048, 512], P(('rep', 'dp')), parts along dimension 0, may hold values from -6 to 6
- new_rope: bfloat16 [2048, 64], P(('rep', 'dp')), parts along dimension 0, may hold values from -6 to 6
- lengths: int32 [2048], P(('rep', 'dp')), parts along dimension 0, may hold values from 1 to 384, as said below
- counts: int32 [256], P(('rep', 'dp')), parts along dimension 0, may hold values from 1 to 8, as said below
- w_uv: bfloat16 [128, 512, 128], P('dp'), may hold values from -0.5 to 0.5
- w_o: bfloat16 [16384, 3584], P('dp'), may hold values from -0.125 to 0.125
- norm_gain: bfloat16 [3584], replicated, may hold values from 0.099609375 to 1.8984375
- w_gate: bfloat16 [3584, 9216], P(None, 'dp'), may hold values from -0.09375 to 0.09375
- w_up: bfloat16 [3584, 9216], P(None, 'dp'), may hold values from -0.09375 to 0.09375
- w_down: bfloat16 [9216, 3584], P('dp'), may hold values from -0.125 to 0.125
Outputs:
- layer_out: bfloat16 [2048, 3584], P(('rep', 'dp')), parts along dimension 0
There are 8 independent parts, one for each index of `rep`. A program takes and returns all parts, laid end to end along the dimension named above; an argument that names none is the same for every part. Nothing has to cross between parts.
Inputs may be any that keep to these rules, and one draw needn't show every extreme that they name: `lengths`: every value at least 1; some live slot of a heavily loaded device holds exactly 384 positions. `counts`: some device has all 8 slots live.
All inputs are finite; a program needn't handle non-finite values.
Results may differ from a plain program's by a relative error of at most 0.024.
Values may be sent and summed in bfloat16 or wider, within the bound.
No kernel may reach another device: no remote copies, remote signals or barrier semaphores. Data moves between devices by JAX's collectives and lax.ppermute only.
A program may use at most 64 MiB of HBM per device.

v0:
```python
import jax
import jax.numpy as jnp
from jax import lax
from jax.sharding import PartitionSpec as P


def normalize(values, gain):
    scaled = values * lax.rsqrt(jnp.mean(values * values, axis=-1, keepdims=True) + 1e-06)
    return (scaled * gain.astype(jnp.float32)).astype(jnp.bfloat16)


def on_device(
    residual_in,
    q_latent,
    q_rope,
    cache_latent,
    cache_rope,
    new_latent,
    new_rope,
    lengths,
    counts,
    w_uv,
    w_o,
    norm_gain,
    w_gate,
    w_up,
    w_down,
):
    row_count = residual_in.shape[0]
    positions = cache_latent.shape[1]
    score_scale = (w_uv.shape[2] + q_rope.shape[1]) ** (-0.5)
    live_slot = jnp.arange(row_count, dtype=jnp.int32) < counts[0]
    used_len = jnp.where(live_slot, lengths, 0)
    scores = jnp.einsum("bhj,bpj->bhp", q_latent, cache_latent, preferred_element_type=jnp.float32)
    scores = scores + jnp.einsum(
        "brh,brp->bhp", q_rope, cache_rope, preferred_element_type=jnp.float32
    )
    scores = scores * score_scale
    fresh_score = (
        jnp.einsum("bhj,bj->bh", q_latent, new_latent, preferred_element_type=jnp.float32)
        + jnp.einsum("brh,br->bh", q_rope, new_rope, preferred_element_type=jnp.float32)
    ) * score_scale
    key_mask = jnp.arange(positions, dtype=jnp.int32)[None, :] < used_len[:, None]
    scores = jnp.where(key_mask[:, None, :], scores, -jnp.inf)
    top = jnp.maximum(jnp.max(scores, axis=2), fresh_score)
    expo = jnp.exp(scores - top[:, :, None])
    fresh_expo = jnp.exp(fresh_score - top)
    total = jnp.sum(expo, axis=2) + fresh_expo
    probs = (expo / total[:, :, None]).astype(jnp.bfloat16)
    fresh_prob = (fresh_expo / total).astype(jnp.bfloat16)
    o_latent = jnp.einsum("bhp,bpj->bhj", probs, cache_latent, preferred_element_type=jnp.float32)
    o_latent = (
        o_latent
        + fresh_prob.astype(jnp.float32)[:, :, None] * new_latent.astype(jnp.float32)[:, None, :]
    )
    o_latent = o_latent.astype(jnp.bfloat16)
    by_head = lax.all_to_all(o_latent, "dp", split_axis=1, concat_axis=0, tiled=True)
    heads_v = jnp.einsum("bhj,hjk->bhk", by_head, w_uv, preferred_element_type=jnp.float32).astype(
        jnp.bfloat16
    )
    flat_heads = heads_v.reshape(heads_v.shape[0], -1)
    picked = flat_heads
    attn_mine = lax.psum_scatter(
        jnp.dot(picked, w_o, preferred_element_type=jnp.float32).astype(jnp.bfloat16),
        "dp",
        scatter_dimension=0,
        tiled=True,
    ).astype(jnp.float32)
    hidden_mine = residual_in.astype(jnp.float32) + attn_mine
    normed_mine = normalize(hidden_mine, norm_gain)
    normed_piece = lax.all_gather(normed_mine, "dp", axis=0, tiled=True)
    gate = jnp.dot(normed_piece, w_gate, preferred_element_type=jnp.float32)
    upper = jnp.dot(normed_piece, w_up, preferred_element_type=jnp.float32)
    activated = (jax.nn.silu(gate) * upper).astype(jnp.bfloat16)
    picked = activated
    ffn_mine = lax.psum_scatter(
        jnp.dot(picked, w_down, preferred_element_type=jnp.float32).astype(jnp.bfloat16),
        "dp",
        scatter_dimension=0,
        tiled=True,
    ).astype(jnp.float32)
    return (hidden_mine + ffn_mine).astype(jnp.bfloat16)


def solution(mesh):
    placed = (
        P(("rep", "dp"), None),
        P(("rep", "dp"), None, None),
        P(("rep", "dp"), None, None),
        P(("rep", "dp"), None, None),
        P(("rep", "dp"), None, None),
        P(("rep", "dp"), None),
        P(("rep", "dp"), None),
        P(("rep", "dp")),
        P(("rep", "dp")),
        P("dp", None, None),
        P("dp", None),
        P(),
        P(None, "dp"),
        P(None, "dp"),
        P("dp", None),
    )
    return jax.shard_map(
        on_device, mesh=mesh, in_specs=placed, out_specs=P(("rep", "dp"), None), check_vma=False
    )
```

profile of v0, /device:TPU:192, one launch (start us, length us, event | category | flops | bytes accessed | tf_op | source)
XLA Modules:
  0.0 280.8 jit_solution(14973182252988821170)
XLA Ops:
  6.5 0.0 reduce-scatter.3.cloned.1.call-start
  7.3 0.8 compare_select_fusion
  8.2 0.1 iota_compare_fusion
  8.2 0.7 convert_element_type.52
  8.9 1.6 fusion.12
  10.5 0.0 copy-start.4
  10.6 2.3 fusion.21
  12.9 0.0 copy-done.5
  12.9 0.1 fusion.14
  13.0 0.5 fusion.20
  13.6 0.5 fusion
  14.1 1.0 add_convert_fusion
  15.1 0.0 copy-start.7
  15.1 0.6 copy.18
  15.7 0.0 copy-start.1
  15.7 24.2 %all_to_all.18 = bf16[8,128,512]{2,0,1:T(8,128)(2,1)S(1)} all-to-all(bf16[8,128,512]{2,0,1:T(8,128)(2,1)S(1)} %copy.18), channel_id=1, replica_groups=mesh['dp'=32,'rep'=8] {'dp'}, dimensions={1} | all-to-all | bytes 2097152 | tf_op jit(solution)/shard_map/all_to_all | solution.py:57
  39.9 0.5 convolution_convert_fusion.2
  40.4 2.4 convolution_convert_fusion.1
  42.8 0.0 reduce-scatter.3.cloned.1.call-update
  42.8 0.0 all-gather.2.cloned.1.call-start
  42.9 0.6 copy-done.6
  43.5 83.2 %reduce-scatter.3.cloned.1.call-done = bf16[8,3584]{1,0:T(8,128)(2,1)} async-done(((bf16[256,3584]{1,0:T(8,128)(2,1)}), bf16[8,3584]{1,0:T(8,128)(2,1)}) %reduce-scatter.3.cloned.1.call-update) | async-done | bytes 57360 | tf_op jit(solution)/shard_map/reduce_scatter | solution.py:63
  126.7 1.0 multiply_reduce_fusion
  127.6 1.5 multiply_convert_fusion
  129.2 0.0 all-gather.2.cloned.1.call-update
  129.2 0.0 reduce-scatter.5.cloned.1.call-start
  129.2 48.1 %all-gather.2.cloned.1.call-done = bf16[256,3584]{1,0:T(8,128)(2,1)} async-done(((bf16[8,3584]{1,0:T(8,128)(2,1)}), bf16[256,3584]{1,0:T(8,128)(2,1)}) %all-gather.2.cloned.1.call-update) | async-done | bytes 1835024 | tf_op jit(solution)/shard_map/all_gather | solution.py:71
  177.3 2.9 %fusion.22 = f32[256,288]{0,1:T(8,128)S(1)} fusion(bf16[256,3584]{1,0:T(8,128)(2,1)} %all-gather.2.cloned.1.call-done, bf16[3584,288]{0,1:T(8,128)(2,1)} %param.27), kind=kOutput, calls=%fused_computation.40 | convolution fusion | flops 528482304 | bytes 4194304 | tf_op jit(solution)/shard_map/dot_general | solution.py:72
  180.2 6.9 %convolution_convert_fusion = bf16[256,3584]{1,0:T(8,128)(2,1)} fusion(bf16[288,3584]{1,0:T(8,128)(2,1)} %param.29, bf16[256,3584]{1,0:T(8,128)(2,1)} %all-gather.2.cloned.1.call-done, bf16[3584,288]{0,1:T(8,128)(2,1)} %param.28, f32[256,288]{0,1:T(8,128)S(1)} %fusion.22), kind=kOutput, calls=%fused_computation | convolution fusion | flops 1058324480 | bytes 8093696 | tf_op jit(solution)/shard_map/dot_general | solution.py:77
  187.1 0.0 reduce-scatter.5.cloned.1.call-update
  187.2 85.6 %reduce-scatter.5.cloned.1.call-done = bf16[8,3584]{1,0:T(8,128)(2,1)} async-done(((bf16[256,3584]{1,0:T(8,128)(2,1)}), bf16[8,3584]{1,0:T(8,128)(2,1)}) %reduce-scatter.5.cloned.1.call-update) | async-done | bytes 57360 | tf_op jit(solution)/shard_map/reduce_scatter | solution.py:76
  272.8 1.5 add_convert_fusion.1
  (17 shorter events, 0.1 us)
Async XLA Ops:
  6.5 4.0 %copy-start = (bf16[8,384,512]{2,1,0:T(8,128)(2,1)S(1)}, bf16[8,384,512]{2,1,0:T(8,128)(2,1)}, u32[]{:S(2)}) copy-start(bf16[8,384,512]{2,1,0:T(8,128)(2,1)} %param.18) | copy-start | bytes 9437188
  6.5 120.1 %reduce-scatter.3.cloned.1.call-start = ((), (), s32[]{:S(2)}) async-start(), calls=%async_computation.3 | async-start | bytes 1892352 | tf_op jit(solution)/shard_map/reduce_scatter | solution.py:63
  10.5 2.4 copy-start.5
  10.5 2.4 copy-start.8
  10.5 2.5 copy-start.4
  15.1 24.8 %copy-start.7 = (bf16[4,512,128]{2,1,0:T(8,128)(2,1)S(1)}, bf16[4,512,128]{2,1,0:T(8,128)(2,1)}, u32[]{:S(2)}) copy-start(bf16[4,512,128]{2,1,0:T(8,128)(2,1)} %param.24) | copy-start | bytes 1572868
  15.7 24.7 %copy-start.1 = (bf16[512,3584]{1,0:T(8,128)(2,1)S(1)}, bf16[512,3584]{1,0:T(8,128)(2,1)}, u32[]{:S(2)}) copy-start(bf16[512,3584]{1,0:T(8,128)(2,1)} %param.25) | copy-start | bytes 11010052
  42.8 0.7 copy-start.6
  42.8 83.9 %copy-start.2 = (bf16[8,3584]{1,0:T(8,128)(2,1)S(1)}, bf16[8,3584]{1,0:T(8,128)(2,1)}, u32[]{:S(2)}) copy-start(bf16[8,3584]{1,0:T(8,128)(2,1)} %param.15) | copy-start | bytes 172036
  42.8 134.5 %all-gather.2.cloned.1.call-start = ((), (), s32[]{:S(2)}) async-start(), calls=%async_computation.4 | async-start | bytes 1892352 | tf_op jit(solution)/shard_map/all_gather | solution.py:71
  129.2 143.6 %reduce-scatter.5.cloned.1.call-start = ((), (), s32[]{:S(2)}) async-start(), calls=%async_computation.5 | async-start | bytes 1892352 | tf_op jit(solution)/shard_map/reduce_scatter | solution.py:76
  187.1 85.6 %copy-start.3 = (bf16[8,3584]{1,0:T(8,128)(2,1)S(1)}, bf16[8,3584]{1,0:T(8,128)(2,1)}, u32[]{:S(2)}) copy-start(bf16[8,3584]{1,0:T(8,128)(2,1)} %reduce-scatter.3.cloned.1.call-done) | copy-start | bytes 172036
Sparse Core Ops, SparseCore 0:
  43.0 83.6 reduce-scatter.2
  129.3 47.9 all-gather.1
  187.3 85.4 reduce-scatter.4
where the time goes:
time: 283 us; the launch traced here: 281 us
  waiting for transfers between devices  217 us (77%)
  blocking collectives  24.2 us (9%)
  matrix products  18.2 us (6%)
  between operations  14 us (5%)
  other arithmetic  6.12 us (2%)
    reduce_scatter x1, waiting for transfers between devices, on_device(): lax.psum_scatter(jnp.dot(picked, w_down, preferred_element_type=jnp.float...  85.6 us
    reduce_scatter x1, waiting for transfers between devices, on_device(): lax.psum_scatter(jnp.dot(picked, w_o, preferred_element_type=jnp.float32)...  83.2 us
    all_gather x1, waiting for transfers between devices, on_device(): normed_piece = lax.all_gather(normed_mine, 'dp', axis=0, tiled=True)  48.1 us
    all_to_all x1, blocking collectives, on_device(): lax.all_to_all(o_latent, 'dp', split_axis=1, concat_axis=0, tiled=True)  24.2 us
    dot_general x1, matrix products, on_device(): jnp.dot(picked, w_down, preferred_element_type=jnp.float32)  6.92 us
  transfers between devices with their start and end apart: 3, of which 3 were waited for; matrix products, arithmetic and copies ran while one was open for 0% of the time, Pallas kernels for 0%

commit v1 on v0

v1 whole, which is shorter than its diff:
```python
import jax
import jax.numpy as jnp
from jax import lax
from jax.sharding import PartitionSpec as P


def normalize(values, gain):
    scaled = values * lax.rsqrt(jnp.mean(values * values, axis=-1, keepdims=True) + 1e-06)
    return (scaled * gain.astype(jnp.float32)).astype(jnp.bfloat16)


def attend(
    q_latent, q_rope, cache_latent, cache_rope, new_latent, new_rope, lengths, counts, score_scale
):
    row_count, positions = cache_latent.shape[:2]
    live_slot = jnp.arange(row_count, dtype=jnp.int32) < counts[0]
    used_len = jnp.where(live_slot, lengths, 0)
    scores = jnp.einsum("bhj,bpj->bhp", q_latent, cache_latent, preferred_element_type=jnp.float32)
    scores = scores + jnp.einsum(
        "brh,brp->bhp", q_rope, cache_rope, preferred_element_type=jnp.float32
    )
    scores = scores * score_scale
    fresh_score = (
        jnp.einsum("bhj,bj->bh", q_latent, new_latent, preferred_element_type=jnp.float32)
        + jnp.einsum("brh,br->bh", q_rope, new_rope, preferred_element_type=jnp.float32)
    ) * score_scale
    key_mask = jnp.arange(positions, dtype=jnp.int32)[None, :] < used_len[:, None]
    scores = jnp.where(key_mask[:, None, :], scores, -jnp.inf)
    top = jnp.maximum(jnp.max(scores, axis=2), fresh_score)
    expo = jnp.exp(scores - top[:, :, None])
    fresh_expo = jnp.exp(fresh_score - top)
    total = jnp.sum(expo, axis=2) + fresh_expo
    probs = (expo / total[:, :, None]).astype(jnp.bfloat16)
    fresh_prob = (fresh_expo / total).astype(jnp.bfloat16)
    o_latent = jnp.einsum("bhp,bpj->bhj", probs, cache_latent, preferred_element_type=jnp.float32)
    o_latent = (
        o_latent
        + fresh_prob.astype(jnp.float32)[:, :, None] * new_latent.astype(jnp.float32)[:, None, :]
    )
    return o_latent.astype(jnp.bfloat16)


def solution(mesh):
    n_dp = mesh.shape["dp"]
    chips = n_dp // 2
    swap = [(i, i ^ 1) for i in range(n_dp)]
    same_core = [[2 * c + k for c in range(chips)] for k in range(2)]

    def sibling(w):
        return lax.ppermute(w, "dp", swap)

    def exchange(v, split_axis=0):
        return lax.all_to_all(
            v, "dp", split_axis, 0, axis_index_groups=same_core, tiled=True
        )

    def summed(part, rows):
        got = exchange(part).reshape(chips, rows, part.shape[-1])
        return jnp.sum(got.astype(jnp.float32), axis=0)

    def dot(a, b):
        return jnp.dot(a, b, preferred_element_type=jnp.float32)

    def on_device(
        residual_in,
        q_latent,
        q_rope,
        cache_latent,
        cache_rope,
        new_latent,
        new_rope,
        lengths,
        counts,
        w_uv,
        w_o,
        norm_gain,
        w_gate,
        w_up,
        w_down,
    ):
        rows = residual_in.shape[0]
        core = lax.axis_index("dp") % 2
        w_uv2, w_o2 = sibling(w_uv), sibling(w_o)
        w_gate2, w_up2, w_down2 = sibling(w_gate), sibling(w_up), sibling(w_down)
        score_scale = (w_uv.shape[2] + q_rope.shape[1]) ** (-0.5)
        o_latent = attend(
            q_latent,
            q_rope,
            cache_latent,
            cache_rope,
            new_latent,
            new_rope,
            lengths,
            counts,
            score_scale,
        )
        by_head = exchange(o_latent, 1)
        heads = w_uv.shape[0]
        first = core == 0
        w_uv_pair = jnp.concatenate(
            [jnp.where(first, w_uv, w_uv2), jnp.where(first, w_uv2, w_uv)], axis=0
        )
        heads_v = jnp.einsum(
            "bhj,hjk->bhk", by_head, w_uv_pair, preferred_element_type=jnp.float32
        ).astype(jnp.bfloat16)
        flat = heads_v.reshape(heads_v.shape[0], -1)
        half = flat.shape[1] // 2
        mine = jnp.where(first, flat[:, :half], flat[:, half:])
        other = jnp.where(first, flat[:, half:], flat[:, :half])
        part = (dot(mine, w_o) + dot(other, w_o2)).astype(jnp.bfloat16)
        hidden_mine = residual_in.astype(jnp.float32) + summed(part, rows)
        normed_mine = normalize(hidden_mine, norm_gain)
        copies = jnp.broadcast_to(normed_mine[None], (chips,) + normed_mine.shape)
        normed = exchange(copies.reshape(chips * rows, -1))

        def activate(gate_w, up_w):
            return (jax.nn.silu(dot(normed, gate_w)) * dot(normed, up_w)).astype(jnp.bfloat16)

        part = (
            dot(activate(w_gate, w_up), w_down) + dot(activate(w_gate2, w_up2), w_down2)
        ).astype(jnp.bfloat16)
        return (hidden_mine + summed(part, rows)).astype(jnp.bfloat16)

    placed = (
        P(("rep", "dp"), None),
        P(("rep", "dp"), None, None),
        P(("rep", "dp"), None, None),
        P(("rep", "dp"), None, None),
        P(("rep", "dp"), None, None),
        P(("rep", "dp"), None),
        P(("rep", "dp"), None),
        P(("rep", "dp")),
        P(("rep", "dp")),
        P("dp", None, None),
        P("dp", None),
        P(),
        P(None, "dp"),
        P(None, "dp"),
        P("dp", None),
    )
    return jax.shard_map(
        on_device, mesh=mesh, in_specs=placed, out_specs=P(("rep", "dp"), None), check_vma=False
    )
```

time: 283 us -> 117 us (0.41)
  waiting for transfers between devices: 217 us -> 28 us
  between operations: 14 us -> 0.99 us
  starting transfers between devices: 0.09 us -> 12.4 us
  matrix products: 18.2 us -> 29.9 us
  blocking collectives: 24.2 us -> 34.2 us
    reduce_scatter x2 -> x0, waiting for transfers between devices: 169 us -> none  [the longest x1 85.6 us: on_device(): lax.psum_scatter(jnp.dot(picked, w_down, preferred_element_type=jnp.float...]
    all_gather x1 -> x0, waiting for transfers between devices: 48.1 us -> none  [on_device(): normed_piece = lax.all_gather(normed_mine, 'dp', axis=0, tiled=True)]
    all_to_all x0 -> x2, waiting for transfers between devices: none -> 25.9 us  [exchange(): lax.all_to_all(v, 'dp', split_axis, 0, axis_index_groups=same_core, tiled...]
    dot_general x9 -> x12, matrix products: 18.2 us -> 29.9 us  [the longest x6 21.6 us: dot(): return jnp.dot(a, b, preferred_element_type=jnp.float32)]
    all_to_all x0 -> x2, starting transfers between devices: none -> 11.5 us  [exchange(): lax.all_to_all(v, 'dp', split_axis, 0, axis_index_groups=same_core, tiled...]
    all_to_all x1 -> x2, blocking collectives: 24.2 us -> 34.2 us  [exchange(): lax.all_to_all(v, 'dp', split_axis, 0, axis_index_groups=same_core, tiled...]
  transfers between devices with their start and end apart: 3 -> 7, of which waited for: 3 -> 3; matrix products, arithmetic and copies ran while one was open for 0% -> 26% of each run, Pallas kernels for 0% -> 0%
where the time goes in v1:
time: 117 us; the launch traced here: 116 us
  blocking collectives  34.2 us (29%)
  matrix products  29.9 us (26%)
  waiting for transfers between devices  28 us (24%)
  starting transfers between devices  12.4 us (11%)
  other arithmetic  6.9 us (6%)
  local copies, waits for them, and re-layouts  3.98 us (3%)
    all_to_all x2, blocking collectives, exchange(): lax.all_to_all(v, 'dp', split_axis, 0, axis_index_groups=same_core, tiled...  34.2 us
    all_to_all x2, waiting for transfers between devices, exchange(): lax.all_to_all(v, 'dp', split_axis, 0, axis_index_groups=same_core, tiled...  25.9 us
    dot_general x6, matrix products, dot(): return jnp.dot(a, b, preferred_element_type=jnp.float32)  21.6 us
    all_to_all x2, starting transfers between devices, exchange(): lax.all_to_all(v, 'dp', split_axis, 0, axis_index_groups=same_core, tiled...  11.5 us
  transfers between devices with their start and end apart: 7, of which 3 were waited for; matrix products, arithmetic and copies ran while one was open for 26% of the time, Pallas kernels for 0%

profile of v1, /device:TPU:192, one launch (start us, length us, event | category | flops | bytes accessed | tf_op | source)
XLA Modules:
  0.0 116.4 jit_solution(17135217737807865306)
XLA Ops:
  0.8 0.8 compare_select_fusion
  1.6 1.0 fusion.44
  2.7 0.7 convert_element_type.55
  3.4 1.6 %fusion.42 = f32[8,1,128]{2,1,0:T(1,128)S(1)} fusion(bf16[8,128,512]{2,1,0:T(8,128)(2,1)} %param.16, bf16[8,512,1]{1,0,2:T(8,128)(2,1)} %bitcast.52), kind=kOutput, calls=%fused_computation.54 | convolution fusion | flops 1048576 | bytes 1060864 | tf_op jit(solution)/shard_map/bhj,bj->bh/dot_general | solution.py:24
  5.1 2.3 %fusion.53 = f32[8,128,384]{2,1,0:T(8,128)S(1)} fusion(bf16[8,128,512]{2,1,0:T(8,128)(2,1)} %param.16, bf16[8,384,512]{2,1,0:T(8,128)(2,1)S(1)} %copy-done), kind=kOutput, calls=%fused_computation.71 | convolution fusion | flops 402653184 | bytes 5767168 | tf_op jit(solution)/shard_map/bhj,bpj->bhp/dot_general | solution.py:18
  7.4 0.5 fusion.52
  7.9 0.5 fusion.4
  8.5 0.9 add_convert_fusion
  9.4 1.6 %copy.23 = bf16[8,128,512]{2,0,1:T(8,128)(2,1)} copy(bf16[8,128,512]{2,1,0:T(8,128)(2,1)S(1)} %add_convert_fusion) | data formatting | bytes 2097152 | tf_op jit(solution)/shard_map/convert_element_type | solution.py:40
  11.0 7.1 %all-to-all-start = ((bf16[8,128,512]{2,0,1:T(8,128)(2,1)}), bf16[8,128,512]{2,0,1:T(8,128)(2,1)}, u32[]{:S(2)}, u32[]{:S(2)}) async-start(bf16[8,128,512]{2,0,1:T(8,128)(2,1)} %copy.23), calls=%async_computation | async-start | bytes 2097152 | tf_op jit(solution)/shard_map/all_to_all | solution.py:53
  18.2 2.1 %copy.21 = bf16[4,512,128]{1,2,0:T(8,128)(2,1)} copy(bf16[4,512,128]{2,1,0:T(8,128)(2,1)} %param.24) | data formatting | bytes 1048576 | tf_op args[9]
  20.2 0.2 collective-permute-start
  20.4 2.1 %collective-permute-done = bf16[4,512,128]{1,2,0:T(8,128)(2,1)} collective-permute-done((bf16[4,512,128]{1,2,0:T(8,128)(2,1)}, bf16[4,512,128]{1,2,0:T(8,128)(2,1)}, u32[]{:S(2)}, u32[]{:S(2)}) %collective-permute-start) | collective-permute-done | bytes 524320 | tf_op jit(solution)/shard_map/ppermute | solution.py:50
  22.5 2.3 %broadcast_select_fusion.1 = (bf16[4,512,128]{1,2,0:T(8,128)(2,1)}, bf16[4,512,128]{1,2,0:T(8,128)(2,1)}) fusion(bf16[4,512,128]{1,2,0:T(8,128)(2,1)} %copy.21, bf16[4,512,128]{1,2,0:T(8,128)(2,1)} %collective-permute-done, pred[]{:T(512)S(6)} %eq.5), kind=kLoop, calls=%fused_computation.32 | loop fusion | flops 524288 | bytes 2097153 | tf_op jit(solution)/shard_map/jit(_where)/select_n | solution.py:101
  24.7 11.9 %all-to-all-done = bf16[8,128,512]{2,0,1:T(8,128)(2,1)} async-done(((bf16[8,128,512]{2,0,1:T(8,128)(2,1)}), bf16[8,128,512]{2,0,1:T(8,128)(2,1)}, u32[]{:S(2)}, u32[]{:S(2)}) %all-to-all-start) | async-done | bytes 1048608 | tf_op jit(solution)/shard_map/all_to_all | solution.py:53
  36.6 2.0 %convolution_convert_fusion = bf16[8,128,128]{2,1,0:T(8,128)(2,1)S(1)} fusion(bf16[4,512,128]{1,2,0:T(8,128)(2,1)} %get-tuple-element.6, bf16[4,512,128]{1,2,0:T(8,128)(2,1)} %get-tuple-element.5, bf16[8,16,8,512]{3,0,2,1:T(8,128)(2,1)} %bitcast.7), kind=kOutput, calls=%fused_computation.13 | convolution fusion | flops 134873088 | bytes 2359296 | tf_op jit(solution)/shard_map/bhj,hjk->bhk/dot_general | solution.py:103
  38.6 2.7 %fusion.28 = f32[128,3584]{1,0:T(8,128)S(1)} fusion(bf16[512,3584]{1,0:T(8,128)(2,1)} %param.25, pred[]{:T(512)S(6)} %eq.5, bf16[128,1024]{0,1:T(8,128)(2,1)S(1)} %bitcast.50), kind=kOutput, calls=%fused_computation.40 | convolution fusion | flops 469827584 | bytes 5767169 | tf_op jit(solution)/shard_map/dot_general | solution.py:62
  41.4 3.7 %fusion.3 = bf16[16,8,3584]{2,1,0:T(8,128)(2,1)} fusion(f32[128,3584]{1,0:T(8,128)S(1)} %fusion.28, bf16[512,3584]{1,0:T(8,128)(2,1)} %collective-permute-done.1, pred[]{:T(512)S(6)} %eq.5, bf16[128,1024]{0,1:T(8,128)(2,1)S(1)} %bitcast.51), kind=kOutput, calls=%fused_computation.5 | convolution fusion | flops 470745088 | bytes 6684673 | tf_op jit(solution)/shard_map/dot_general | solution.py:62
  45.0 4.4 %all-to-all-start.1 = ((bf16[16,8,3584]{2,1,0:T(8,128)(2,1)}), bf16[16,8,3584]{2,1,0:T(8,128)(2,1)}, u32[]{:S(2)}, u32[]{:S(2)}) async-start(bf16[16,8,3584]{2,1,0:T(8,128)(2,1)} %fusion.3), calls=%async_computation.1 | async-start | bytes 1835008 | tf_op jit(solution)/shard_map/all_to_all | solution.py:53
  49.6 0.5 collective-permute-start.2
  50.2 14.0 %all-to-all-done.1 = bf16[16,8,3584]{2,1,0:T(8,128)(2,1)} async-done(((bf16[16,8,3584]{2,1,0:T(8,128)(2,1)}), bf16[16,8,3584]{2,1,0:T(8,128)(2,1)}, u32[]{:S(2)}, u32[]{:S(2)}) %all-to-all-start.1) | async-done | bytes 917536 | tf_op jit(solution)/shard_map/all_to_all | solution.py:53
  64.2 1.5 %convert_reduce_fusion.1 = f32[8,3584]{1,0:T(8,128)S(1)} fusion(bf16[16,8,3584]{2,1,0:T(8,128)(2,1)} %all-to-all-done.1), kind=kLoop, calls=%fused_computation.8 | loop fusion | flops 888832 | bytes 1032192 | tf_op jit(solution)/shard_map/reduce_sum | solution.py:59
  65.7 0.1 multiply_reduce_fusion
  66.0 17.4 %all_to_all.45 = bf16[16,8,3584]{2,1,0:T(8,128)(2,1)S(1)} all-to-all(bf16[16,8,3584]{2,1,0:T(8,128)(2,1)S(1)} %broadcast_in_dim.21), channel_id=1, replica_groups={{0,16,32,48,64,80,96,112,128,144,160,176,192,208,224,240},{8,24,40,56,7..., dimensions={0} | all-to-all | bytes 1835008 | tf_op jit(solution)/shard_map/all_to_all | solution.py:53
  83.4 0.7 fusion.18
  84.1 0.2 copy-done.1
  84.4 2.3 %fusion.12 = f32[128,288]{0,1:T(8,128)S(1)} fusion(bf16[3584,288]{0,1:T(8,128)(2,1)} %collective-permute-done.3, bf16[16,8,3584]{2,1,0:T(8,128)(2,1)S(1)} %all_to_all.45), kind=kOutput, calls=%fused_computation.22 | convolution fusion | flops 264241152 | bytes 3129344 | tf_op jit(solution)/shard_map/dot_general | solution.py:62
  86.6 6.0 %fusion.6 = f32[128,3584]{1,0:T(8,128)} fusion(bf16[288,3584]{1,0:T(8,128)(2,1)} %param.29, bf16[3584,288]{0,1:T(8,128)(2,1)} %param.28, bf16[16,8,3584]{2,1,0:T(8,128)(2,1)} %copy-done.1, f32[128,288]{0,1:T(8,128)S(1)} %fusion.18), kind=kOutput, calls=%fused_computation.16 | convolution fusion | flops 528703488 | bytes 7028736 | tf_op jit(solution)/shard_map/dot_general | solution.py:62
  92.7 6.2 %fusion.2 = bf16[16,8,3584]{2,1,0:T(8,128)(2,1)} fusion(f32[128,3584]{1,0:T(8,128)} %fusion.6, bf16[288,3584]{1,0:T(8,128)(2,1)} %collective-permute-done.4, f32[128,288]{0,1:T(8,128)S(1)} %fusion.12, bf16[3584,288]{0,1:T(8,128)(2,1)} %collective-permute-done.2, bf16[16,8,3584]{2,1,0:T(8,128)(2,1)} %copy-done.1), kind=kOutput, calls=%fused_computation.4 | convolution fusion | flops 529620992 | bytes 7946240 | tf_op jit(solution)/shard_map/dot_general | solution.py:62
  98.9 16.7 %all_to_all.46 = bf16[16,8,3584]{2,1,0:T(8,128)(2,1)S(1)} all-to-all(bf16[16,8,3584]{2,1,0:T(8,128)(2,1)} %fusion.2), channel_id=1, replica_groups={{0,16,32,48,64,80,96,112,128,144,160,176,192,208,224,240},{8,24,40,56,7..., dimensions={0} | all-to-all | bytes 1835008 | tf_op jit(solution)/shard_map/all_to_all | solution.py:53
  115.6 0.1 convert_reduce_fusion
  115.8 0.6 add_convert_fusion.1
  (29 shorter events, 0.5 us)
Async XLA Ops:
  0.0 5.0 %copy-start = (bf16[8,384,512]{2,1,0:T(8,128)(2,1)S(1)}, bf16[8,384,512]{2,1,0:T(8,128)(2,1)}, u32[]{:S(2)}) copy-start(bf16[8,384,512]{2,1,0:T(8,128)(2,1)} %param.18) | copy-start | bytes 9437188
  0.0 41.4 %collective-permute-start.1 = (bf16[512,3584]{1,0:T(8,128)(2,1)}, bf16[512,3584]{1,0:T(8,128)(2,1)}, u32[]{:S(2)}, u32[]{:S(2)}) collective-permute-start(bf16[512,3584]{1,0:T(8,128)(2,1)} %param.25), channel_id=1, source_target_pairs={{0,8},{8,0},{16,24},{24,16},{32,40},{40,32},{48,56},{56,48},{64,72... | collective-permute-start | bytes 11010056 | tf_op jit(solution)/shard_map/ppermute | solution.py:50
  5.0 2.4 %copy-start.5 = (bf16[8,64,384]{2,1,0:T(8,128)(2,1)S(1)}, bf16[8,64,384]{2,1,0:T(8,128)(2,1)}, u32[]{:S(2)}) copy-start(bf16[8,64,384]{2,1,0:T(8,128)(2,1)} %param.19) | copy-start | bytes 1179652
  5.0 2.4 %copy-start.6 = (bf16[8,64,128]{2,1,0:T(8,128)(2,1)S(1)}, bf16[8,64,128]{2,1,0:T(8,128)(2,1)}, u32[]{:S(2)}) copy-start(bf16[8,64,128]{2,1,0:T(8,128)(2,1)} %param.17) | copy-start | bytes 393220
  11.0 25.6 %all-to-all-start = ((bf16[8,128,512]{2,0,1:T(8,128)(2,1)}), bf16[8,128,512]{2,0,1:T(8,128)(2,1)}, u32[]{:S(2)}, u32[]{:S(2)}) async-start(bf16[8,128,512]{2,0,1:T(8,128)(2,1)} %copy.23), calls=%async_computation | async-start | bytes 2097152 | tf_op jit(solution)/shard_map/all_to_all | solution.py:53
  20.2 2.3 %collective-permute-start = (bf16[4,512,128]{1,2,0:T(8,128)(2,1)}, bf16[4,512,128]{1,2,0:T(8,128)(2,1)}, u32[]{:S(2)}, u32[]{:S(2)}) collective-permute-start(bf16[4,512,128]{1,2,0:T(8,128)(2,1)} %copy.21), channel_id=1, source_target_pairs={{0,8},{8,0},{16,24},{24,16},{32,40},{40,32},{48,56},{56,48},{64,72... | collective-permute-start | bytes 1572872 | tf_op jit(solution)/shard_map/ppermute | solution.py:50
  41.4 8.8 %copy-start.7 = (bf16[3584]{0:T(1024)(128)(2,1)S(1)}, bf16[3584]{0:T(1024)(128)(2,1)}, u32[]{:S(2)}) copy-start(bf16[3584]{0:T(1024)(128)(2,1)} %param.26) | copy-start | bytes 21508
  45.0 20.6 %copy-start.3 = (bf16[8,3584]{1,0:T(8,128)(2,1)S(1)}, bf16[8,3584]{1,0:T(8,128)(2,1)}, u32[]{:S(2)}) copy-start(bf16[8,3584]{1,0:T(8,128)(2,1)} %param.15) | copy-start | bytes 172036
  45.0 19.2 %all-to-all-start.1 = ((bf16[16,8,3584]{2,1,0:T(8,128)(2,1)}), bf16[16,8,3584]{2,1,0:T(8,128)(2,1)}, u32[]{:S(2)}, u32[]{:S(2)}) async-start(bf16[16,8,3584]{2,1,0:T(8,128)(2,1)} %fusion.3), calls=%async_computation.1 | async-start | bytes 1835008 | tf_op jit(solution)/shard_map/all_to_all | solution.py:53
  49.5 34.6 %collective-permute-start.3 = (bf16[3584,288]{0,1:T(8,128)(2,1)}, bf16[3584,288]{0,1:T(8,128)(2,1)}, u32[]{:S(2)}, u32[]{:S(2)}) collective-permute-start(bf16[3584,288]{0,1:T(8,128)(2,1)} %param.28), channel_id=1, source_target_pairs={{0,8},{8,0},{16,24},{24,16},{32,40},{40,32},{48,56},{56,48},{64,72... | collective-permute-start | bytes 6193160 | tf_op jit(solution)/shard_map/ppermute | solution.py:50
  49.6 43.1 %collective-permute-start.2 = (bf16[3584,288]{0,1:T(8,128)(2,1)}, bf16[3584,288]{0,1:T(8,128)(2,1)}, u32[]{:S(2)}, u32[]{:S(2)}) collective-permute-start(bf16[3584,288]{0,1:T(8,128)(2,1)} %param.27), channel_id=1, source_target_pairs={{0,8},{8,0},{16,24},{24,16},{32,40},{40,32},{48,56},{56,48},{64,72... | collective-permute-start | bytes 6193160 | tf_op jit(solution)/shard_map/ppermute | solution.py:50
  50.1 42.6 %collective-permute-start.4 = (bf16[288,3584]{1,0:T(8,128)(2,1)}, bf16[288,3584]{1,0:T(8,128)(2,1)}, u32[]{:S(2)}, u32[]{:S(2)}) collective-permute-start(bf16[288,3584]{1,0:T(8,128)(2,1)} %param.29), channel_id=1, source_target_pairs={{0,8},{8,0},{16,24},{24,16},{32,40},{40,32},{48,56},{56,48},{64,72... | collective-permute-start | bytes 6193160 | tf_op jit(solution)/shard_map/ppermute | solution.py:50
  64.2 19.2 %copy-start.2 = (bf16[3584,288]{0,1:T(8,128)(2,1)S(1)}, bf16[3584,288]{0,1:T(8,128)(2,1)}, u32[]{:S(2)}) copy-start(bf16[3584,288]{0,1:T(8,128)(2,1)} %param.27) | copy-start | bytes 6193156
  83.4 0.9 copy-start.1
  98.9 16.9 %copy-start.4 = (bf16[8,3584]{1,0:T(8,128)(2,1)S(1)}, bf16[8,3584]{1,0:T(8,128)(2,1)}, u32[]{:S(2)}) copy-start(bf16[8,3584]{1,0:T(8,128)(2,1)} %param.15) | copy-start | bytes 172036

commit v2 on v1

v2 whole, which is shorter than its diff:
```python
import jax
import jax.numpy as jnp
from jax import lax
from jax.experimental import pallas as pl
from jax.experimental.pallas import tpu as pltpu
from jax.sharding import PartitionSpec as P

F32, BF16 = jnp.float32, jnp.bfloat16
VMEM_BYTES = 40 * 2**20
HBM = pl.BlockSpec(memory_space=pl.ANY)
VMEM = pl.BlockSpec(memory_space=pltpu.VMEM)
SMEM = pl.BlockSpec(memory_space=pltpu.SMEM)


def normalize(values, gain):
    scaled = values * lax.rsqrt(jnp.mean(values * values, axis=-1, keepdims=True) + 1e-06)
    return (scaled * gain.astype(F32)).astype(BF16)


def mul(a, b, a_dim=1, b_dim=0):
    return lax.dot_general(a, b, (((a_dim,), (b_dim,)), ((), ())), preferred_element_type=F32)


def cost(flops, size):
    return pl.CostEstimate(flops=flops, bytes_accessed=size, transcendentals=0)


def attend_kernel(
    scale,
    lengths_ref,
    counts_ref,
    new_latent_ref,
    new_rope_ref,
    q_latent_hbm,
    q_rope_hbm,
    cache_latent_hbm,
    cache_rope_hbm,
    out_ref,
    q_lat,
    q_rot,
    c_lat,
    c_rot,
    acc,
    sems,
):
    rows, heads, width = q_lat.shape
    positions = c_lat.shape[1]
    pairs = (
        (q_latent_hbm, q_lat),
        (cache_latent_hbm, c_lat),
        (q_rope_hbm, q_rot),
        (cache_rope_hbm, c_rot),
    )
    copies = [
        [
            pltpu.make_async_copy(src.at[t], dst.at[t], sems.at[t, i])
            for i, (src, dst) in enumerate(pairs)
        ]
        for t in range(rows)
    ]
    for group in copies:
        for c in group:
            c.start()
    position = lax.broadcasted_iota(jnp.int32, (heads, positions), 1)
    fresh_lat = new_latent_ref[...]
    fresh_rot = new_rope_ref[...]
    for t in range(rows):
        for c in copies[t]:
            c.wait()
        used = jnp.where(t < counts_ref[0], lengths_ref[t], 0)
        q = q_lat[t]
        rot = q_rot[t].T
        keys = c_lat[t]
        scores = (mul(q, keys, 1, 1) + mul(rot, c_rot[t])) * scale
        fresh = ((mul(q, fresh_lat, 1, 1) + mul(rot, fresh_rot, 1, 1)) * scale)[:, t : t + 1]
        scores = jnp.where(position < used, scores, -jnp.inf)
        top = jnp.maximum(jnp.max(scores, axis=1, keepdims=True), fresh)
        expo = jnp.exp(scores - top)
        fresh_expo = jnp.exp(fresh - top)
        inverse = 1.0 / (jnp.sum(expo, axis=1, keepdims=True) + fresh_expo)
        probs = (expo * inverse).astype(BF16)
        fresh_prob = (fresh_expo * inverse).astype(BF16).astype(F32)
        o = mul(probs, keys) + fresh_prob * fresh_lat[t : t + 1].astype(F32)
        for j in range(width // 128):
            acc[j, pl.ds(t, heads, stride=rows), :] = o[:, j * 128 : (j + 1) * 128]
    for j in range(width // 128):
        out_ref[:, j * 128 : (j + 1) * 128] = acc[j].astype(BF16)


def attend(scale, q_latent, q_rope, cache_latent, cache_rope, new_latent, new_rope, lengths, counts):
    rows, heads, width = q_latent.shape
    positions = cache_latent.shape[1]

    def body(*refs):
        attend_kernel(scale, *refs)

    size = 2 * (q_latent.size * 2 + cache_latent.size + q_rope.size + cache_rope.size)
    flops = 4 * rows * heads * positions * width
    return pl.pallas_call(
        body,
        out_shape=jax.ShapeDtypeStruct((heads * rows, width), BF16),
        in_specs=[SMEM, SMEM, VMEM, VMEM, HBM, HBM, HBM, HBM],
        out_specs=VMEM,
        scratch_shapes=[
            pltpu.VMEM(q_latent.shape, BF16),
            pltpu.VMEM(q_rope.shape, BF16),
            pltpu.VMEM(cache_latent.shape, BF16),
            pltpu.VMEM(cache_rope.shape, BF16),
            pltpu.VMEM((width // 128, heads * rows, 128), F32),
            pltpu.SemaphoreType.DMA((rows, 4)),
        ],
        compiler_params=pltpu.CompilerParams(vmem_limit_bytes=VMEM_BYTES),
        cost_estimate=cost(flops, size),
        name="attend",
    )(lengths, counts, new_latent, new_rope, q_latent, q_rope, cache_latent, cache_rope)


def project_kernel(
    block,
    core_ref,
    got_hbm,
    uv_hbm,
    uv2_hbm,
    o_hbm,
    o2_hbm,
    out_ref,
    got,
    uv,
    uv2,
    wo,
    wo2,
    heads_v,
    sems,
):
    chips, span, width = got.shape
    heads = uv.shape[0]
    hv = uv.shape[2]
    rows = span // (2 * heads)
    cols = wo.shape[1]
    first = [
        pltpu.make_async_copy(src, dst, sems.at[i])
        for i, (src, dst) in enumerate(((got_hbm, got), (uv_hbm, uv), (uv2_hbm, uv2)))
    ]
    later = []
    for n in range(cols // block):
        at = pl.ds(n * block, block)
        later.append(
            [
                pltpu.make_async_copy(o_hbm.at[:, at], wo.at[:, at], sems.at[3 + 2 * n]),
                pltpu.make_async_copy(o2_hbm.at[:, at], wo2.at[:, at], sems.at[4 + 2 * n]),
            ]
        )
    for c in first:
        c.start()
    for group in later:
        for c in group:
            c.start()
    for c in first:
        c.wait()
    core = core_ref[0]
    half = heads * rows
    for s, w in enumerate((uv, uv2)):
        which = core if s == 0 else 1 - core
        mine = got[:, pl.ds(pl.multiple_of(which * half, half), half), :].astype(F32)
        for i in range(heads):
            x = mine[:, i * rows : (i + 1) * rows, :].reshape(chips * rows, width).astype(BF16)
            heads_v[s, :, i * hv : (i + 1) * hv] = mul(x, w[i]).astype(BF16)
    a, b = heads_v[0], heads_v[1]
    for n in range(cols // block):
        for c in later[n]:
            c.wait()
        at = slice(n * block, (n + 1) * block)
        out_ref[:, at] = (mul(a, wo[:, at]) + mul(b, wo2[:, at])).astype(BF16)


def project(core, got, w_uv, w_uv2, w_o, w_o2):
    chips, span, width = got.shape
    heads = w_uv.shape[0]
    rows = chips * span // (2 * heads)
    cols = w_o.shape[1]
    block = 512

    def body(*refs):
        project_kernel(block, *refs)

    size = 2 * (got.size + 2 * w_uv.size + 2 * w_o.size + rows * cols)
    return pl.pallas_call(
        body,
        out_shape=jax.ShapeDtypeStruct((rows, cols), BF16),
        in_specs=[SMEM, HBM, HBM, HBM, HBM, HBM],
        out_specs=VMEM,
        scratch_shapes=[
            pltpu.VMEM(got.shape, BF16),
            pltpu.VMEM(w_uv.shape, BF16),
            pltpu.VMEM(w_uv.shape, BF16),
            pltpu.VMEM(w_o.shape, BF16),
            pltpu.VMEM(w_o.shape, BF16),
            pltpu.VMEM((2, rows, w_o.shape[0]), BF16),
            pltpu.SemaphoreType.DMA((3 + 2 * (cols // block),)),
        ],
        compiler_params=pltpu.CompilerParams(vmem_limit_bytes=VMEM_BYTES),
        cost_estimate=cost(4 * rows * w_o.size, size),
        name="project",
    )(core, got, w_uv, w_uv2, w_o, w_o2)


def feed_kernel(block, x_ref, *refs):
    weights, (out_ref,), (scratch, sems) = refs[:6], refs[6:7], refs[7:]
    copies = [pltpu.make_async_copy(w, scratch.at[i], sems.at[i]) for i, w in enumerate(weights)]
    for c in copies:
        c.start()
    x = x_ref[...]
    activated = []
    for s in range(2):
        copies[2 * s].wait()
        gate = mul(x, scratch[2 * s], 1, 1)
        copies[2 * s + 1].wait()
        upper = mul(x, scratch[2 * s + 1], 1, 1)
        activated.append((gate / (1.0 + jnp.exp(-gate)) * upper).astype(BF16))
    copies[4].wait()
    copies[5].wait()
    cols = out_ref.shape[1]
    for n in range(cols // block):
        at = slice(n * block, (n + 1) * block)
        out_ref[:, at] = (
            mul(activated[0], scratch[4, :, at]) + mul(activated[1], scratch[5, :, at])
        ).astype(BF16)


def feed(x, *weights):
    rows, cols = x.shape

    def body(*refs):
        feed_kernel(512, *refs)

    size = 2 * (2 * x.size + sum(w.size for w in weights))
    return pl.pallas_call(
        body,
        out_shape=jax.ShapeDtypeStruct((rows, cols), BF16),
        in_specs=[VMEM] + [HBM] * 6,
        out_specs=VMEM,
        scratch_shapes=[
            pltpu.VMEM((6,) + weights[0].shape, BF16),
            pltpu.SemaphoreType.DMA((6,)),
        ],
        compiler_params=pltpu.CompilerParams(vmem_limit_bytes=VMEM_BYTES),
        cost_estimate=cost(12 * rows * weights[0].size, size),
        name="feed",
    )(x, *weights)


def solution(mesh):
    n_dp = mesh.shape["dp"]
    chips = n_dp // 2
    swap = [(i, i ^ 1) for i in range(n_dp)]
    same_core = [[2 * c + k for c in range(chips)] for k in range(2)]

    def sibling(w):
        return lax.ppermute(w, "dp", swap)

    def exchange(v):
        return lax.all_to_all(v, "dp", 0, 0, axis_index_groups=same_core, tiled=True)

    def summed(part, rows):
        got = exchange(part).reshape(chips, rows, part.shape[-1])
        return jnp.sum(got.astype(F32), axis=0)

    def on_device(
        residual_in,
        q_latent,
        q_rope,
        cache_latent,
        cache_rope,
        new_latent,
        new_rope,
        lengths,
        counts,
        w_uv,
        w_o,
        norm_gain,
        w_gate,
        w_up,
        w_down,
    ):
        rows = residual_in.shape[0]
        core = (lax.axis_index("dp") % 2).astype(jnp.int32).reshape(1)
        gate_t, up_t = w_gate.T, w_up.T
        w_uv2, w_o2 = sibling(w_uv), sibling(w_o)
        gate2, up2, down2 = sibling(gate_t), sibling(up_t), sibling(w_down)
        scale = (w_uv.shape[2] + q_rope.shape[1]) ** (-0.5)
        o_latent = attend(
            scale, q_latent, q_rope, cache_latent, cache_rope, new_latent, new_rope, lengths, counts
        )
        got = exchange(o_latent).reshape(chips, -1, o_latent.shape[1])
        part = project(core, got, w_uv, w_uv2, w_o, w_o2)
        hidden_mine = residual_in.astype(F32) + summed(part, rows)
        normed_mine = normalize(hidden_mine, norm_gain)
        copies = jnp.broadcast_to(normed_mine[None], (chips,) + normed_mine.shape)
        normed = exchange(copies.reshape(chips * rows, -1))
        part = feed(normed, gate_t, up_t, gate2, up2, w_down, down2)
        return (hidden_mine + summed(part, rows)).astype(BF16)

    placed = (
        P(("rep", "dp"), None),
        P(("rep", "dp"), None, None),
        P(("rep", "dp"), None, None),
        P(("rep", "dp"), None, None),
        P(("rep", "dp"), None, None),
        P(("rep", "dp"), None),
        P(("rep", "dp"), None),
        P(("rep", "dp")),
        P(("rep", "dp")),
        P("dp", None, None),
        P("dp", None),
        P(),
        P(None, "dp"),
        P(None, "dp"),
        P("dp", None),
    )
    return jax.shard_map(
        on_device, mesh=mesh, in_specs=placed, out_specs=P(("rep", "dp"), None), check_vma=False
    )
```

time: 117 us -> 122 us (1.043)
  matrix products: 29.9 us -> 0 us
  Pallas kernels: 0 us -> 24.2 us
  waiting for transfers between devices: 28 us -> 45.5 us
  blocking collectives: 34.2 us -> 17.6 us
  local copies, waits for them, and re-layouts: 3.98 us -> 16.1 us
  other arithmetic: 6.9 us -> 1.13 us
  starting transfers between devices: 12.4 us -> 15.8 us
    dot_general x12 -> x0, matrix products: 29.9 us -> none  [the longest x6 21.6 us: dot(): return jnp.dot(a, b, preferred_element_type=jnp.float32)]
    pallas_call x0 -> x3, Pallas kernels: none -> 24.2 us  [the longest x1 12.6 us: attend(): pl.pallas_call(body, out_shape=jax.ShapeDtypeStruct((heads * rows, width)...]
    all_to_all x2 -> x3, waiting for transfers between devices: 25.9 us -> 43.8 us  [exchange(): lax.all_to_all(v, 'dp', 0, 0, axis_index_groups=same_core, tiled=True)]
    all_to_all x2 -> x1, blocking collectives: 34.2 us -> 17.6 us  [exchange(): lax.all_to_all(v, 'dp', 0, 0, axis_index_groups=same_core, tiled=True)]
    unnamed x17 -> x34, local copies, waits for them, and re-layouts: 2.31 us -> 15.1 us
    all_to_all x2 -> x3, starting transfers between devices: 11.5 us -> 14.8 us  [exchange(): lax.all_to_all(v, 'dp', 0, 0, axis_index_groups=same_core, tiled=True)]
    select_n x2 -> x0, other arithmetic: 3.07 us -> none  [the longest x1 2.26 us: on_device(): jnp.where(first, w_uv, w_uv2)]
    reduce_sum x3 -> x2, other arithmetic: 2.13 us -> 0.25 us  [summed(): return jnp.sum(got.astype(F32), axis=0)]
  transfers between devices with their start and end apart: 7 -> 8, of which waited for: 3 -> 4; matrix products, arithmetic and copies ran while one was open for 26% -> 1% of each run, Pallas kernels for 0% -> 10%
where the time goes in v2:
time: 122 us; the launch traced here: 121 us
  waiting for transfers between devices  45.5 us (37%)
  Pallas kernels  24.2 us (20%)
  blocking collectives  17.6 us (14%)
  local copies, waits for them, and re-layouts  16.1 us (13%)
  starting transfers between devices  15.8 us (13%)
    all_to_all x3, waiting for transfers between devices, exchange(): lax.all_to_all(v, 'dp', 0, 0, axis_index_groups=same_core, tiled=True)  43.8 us
    all_to_all x1, blocking collectives, exchange(): lax.all_to_all(v, 'dp', 0, 0, axis_index_groups=same_core, tiled=True)  17.6 us
    unnamed x34, local copies, waits for them, and re-layouts  15.1 us
    all_to_all x3, starting transfers between devices, exchange(): lax.all_to_all(v, 'dp', 0, 0, axis_index_groups=same_core, tiled=True)  14.8 us
    pallas_call x1, Pallas kernels, attend(): pl.pallas_call(body, out_shape=jax.ShapeDtypeStruct((heads * rows, width)...  12.6 us
    pallas_call x1, Pallas kernels, feed(): pl.pallas_call(body, out_shape=jax.ShapeDtypeStruct((rows, cols), BF16),...  7.01 us
    pallas_call x1, Pallas kernels, project(): pl.pallas_call(body, out_shape=jax.ShapeDtypeStruct((rows, cols), BF16),...  4.61 us
  transfers between devices with their start and end apart: 8, of which 4 were waited for; matrix products, arithmetic and copies ran while one was open for 1% of the time, Pallas kernels for 10%

profile of v2, /device:TPU:192, one launch (start us, length us, event | category | flops | bytes accessed | tf_op | source)
XLA Modules:
  0.0 121.1 jit_solution(17775586610305981920)
XLA Ops:
  0.7 1.9 %copy-done.1 = bf16[8,384,512]{2,1,0:T(8,128)(2,1)S(1)} copy-done((bf16[8,384,512]{2,1,0:T(8,128)(2,1)S(1)}, bf16[8,384,512]{2,1,0:T(8,128)(2,1)}, u32[]{:S(2)}) %copy-start.1) | copy-done | bytes 3145752
  2.5 1.2 %copy-done.5 = bf16[8,128,512]{2,1,0:T(8,128)(2,1)S(1)} copy-done((bf16[8,128,512]{2,1,0:T(8,128)(2,1)S(1)}, bf16[8,128,512]{2,1,0:T(8,128)(2,1)}, u32[]{:S(2)}) %copy-start.5) | copy-done | bytes 1048600
  3.8 1.0 copy-done.10
  4.8 0.9 copy-done.11
  5.7 0.7 copy-done.12
  6.4 0.7 copy-done.13
  7.1 0.7 copy-done.14
  7.7 12.6 %attend.1 = bf16[1024,512]{1,0:T(8,128)(2,1)} custom-call(s32[8]{0:T(128)S(1)} %copy-done.14, s32[1]{0:T(128)S(6)} %copy.16.refs_1_, bf16[8,512]{1,0:T(8,128)(2,1)S(1)} %copy-done.12, bf16[8,64]{1,0:T(8,128)(2,1)S(1)} %copy-done.13, bf16[8,128,512]{2,1,0:T(8,128)(2,1)S(1)} %copy-done.5, bf16[8,64,128]{2,1,0:T(8,128)(2,1)S(1)} %copy-done.11, ...), custom_call_target="tpu_custom_call" | custom-call | flops 805306368 | bytes 5767168 | tf_op jit(solution)/shard_map/attend/pallas_call | solution.py:99
  20.3 7.2 %all-to-all-start = ((bf16[16,64,512]{2,1,0:T(8,128)(2,1)}), bf16[16,64,512]{2,1,0:T(8,128)(2,1)S(1)}, u32[]{:S(2)}, u32[]{:S(2)}) async-start(bf16[16,64,512]{2,1,0:T(8,128)(2,1)} %bitcast.1), calls=%async_computation | async-start | bytes 2097152 | tf_op jit(solution)/shard_map/all_to_all | solution.py:262
  27.5 0.3 collective-permute-start
  27.8 1.7 %collective-permute-done.refs_3_ = bf16[4,512,128]{2,1,0:T(8,128)(2,1)S(1)} collective-permute-done((bf16[4,512,128]{2,1,0:T(8,128)(2,1)S(1)}, bf16[4,512,128]{2,1,0:T(8,128)(2,1)S(1)}, u32[]{:S(2)}, u32[]{:S(2)}) %collective-permute-start) | collective-permute-done | bytes 524320 | tf_op jit(solution)/shard_map/ppermute | solution.py:259
  29.5 0.8 copy-done.8
  30.3 15.7 %all-to-all-done.refs_1_ = bf16[16,64,512]{2,1,0:T(8,128)(2,1)S(1)} async-done(((bf16[16,64,512]{2,1,0:T(8,128)(2,1)}), bf16[16,64,512]{2,1,0:T(8,128)(2,1)S(1)}, u32[]{:S(2)}, u32[]{:S(2)}) %all-to-all-start) | async-done | bytes 1048608 | tf_op jit(solution)/shard_map/all_to_all | solution.py:262
  46.0 2.0 %copy-done = bf16[512,3584]{1,0:T(8,128)(2,1)S(1)} copy-done((bf16[512,3584]{1,0:T(8,128)(2,1)S(1)}, bf16[512,3584]{1,0:T(8,128)(2,1)}, u32[]{:S(2)}) %copy-start) | copy-done | bytes 3670040
  48.0 1.0 copy-done.7
  49.1 1.0 copy-done.9
  50.1 4.6 %project.1 = bf16[128,3584]{1,0:T(8,128)(2,1)} custom-call(s32[1]{0:T(128)} %bitcast.refs_0_, bf16[16,64,512]{2,1,0:T(8,128)(2,1)S(1)} %all-to-all-done.refs_1_, bf16[4,512,128]{2,1,0:T(8,128)(2,1)S(1)} %copy-done.7, bf16[4,512,128]{2,1,0:T(8,128)(2,1)S(1)} %copy-done.9, bf16[512,3584]{1,0:T(8,128)(2,1)S(1)} %copy-done, ...), custom_call_target="tpu_custom_call" | custom-call | flops 939524096 | bytes 10354688 | tf_op jit(solution)/shard_map/project/pallas_call | solution.py:187
  54.7 3.8 %all-to-all-start.1 = ((bf16[16,8,3584]{2,1,0:T(8,128)(2,1)}), bf16[16,8,3584]{2,1,0:T(8,128)(2,1)S(1)}, u32[]{:S(2)}, u32[]{:S(2)}) async-start(bf16[16,8,3584]{2,1,0:T(8,128)(2,1)} %bitcast.2), calls=%async_computation.1 | async-start | bytes 1835008 | tf_op jit(solution)/shard_map/all_to_all | solution.py:262
  58.6 0.5 collective-permute-start.3
  59.1 0.1 collective-permute-start.4
  59.2 14.2 %all-to-all-done.1 = bf16[16,8,3584]{2,1,0:T(8,128)(2,1)S(1)} async-done(((bf16[16,8,3584]{2,1,0:T(8,128)(2,1)}), bf16[16,8,3584]{2,1,0:T(8,128)(2,1)S(1)}, u32[]{:S(2)}, u32[]{:S(2)}) %all-to-all-start.1) | async-done | bytes 917536 | tf_op jit(solution)/shard_map/all_to_all | solution.py:262
  73.4 0.1 convert_reduce_fusion.1
  73.5 0.1 multiply_reduce_fusion
  73.8 1.0 broadcast_in_dim.2
  74.8 3.8 %all-to-all-start.2 = ((bf16[16,8,3584]{2,1,0:T(8,128)(2,1)}), bf16[16,8,3584]{2,1,0:T(8,128)(2,1)S(1)}, u32[]{:S(2)}, u32[]{:S(2)}) async-start(bf16[16,8,3584]{2,1,0:T(8,128)(2,1)} %broadcast_in_dim.2), calls=%async_computation.2 | async-start | bytes 1835008 | tf_op jit(solution)/shard_map/all_to_all | solution.py:262
  78.6 13.9 %all-to-all-done.2 = bf16[16,8,3584]{2,1,0:T(8,128)(2,1)S(1)} async-done(((bf16[16,8,3584]{2,1,0:T(8,128)(2,1)}), bf16[16,8,3584]{2,1,0:T(8,128)(2,1)S(1)}, u32[]{:S(2)}, u32[]{:S(2)}) %all-to-all-start.2) | async-done | bytes 917536 | tf_op jit(solution)/shard_map/all_to_all | solution.py:262
  92.6 1.6 %copy-done.3 = bf16[3584,288]{0,1:T(8,128)(2,1)S(1)} copy-done((bf16[3584,288]{0,1:T(8,128)(2,1)S(1)}, bf16[3584,288]{0,1:T(8,128)(2,1)}, u32[]{:S(2)}) %copy-start.3) | copy-done | bytes 2064408
  94.2 1.6 %copy-done.4 = bf16[288,3584]{1,0:T(8,128)(2,1)S(1)} copy-done((bf16[288,3584]{1,0:T(8,128)(2,1)S(1)}, bf16[288,3584]{1,0:T(8,128)(2,1)}, u32[]{:S(2)}) %copy-start.4) | copy-done | bytes 2064408
  95.7 7.0 %feed.1 = bf16[128,3584]{1,0:T(8,128)(2,1)S(1)} custom-call(bf16[128,3584]{1,0:T(8,128)(2,1)S(1)} %bitcast.7, bf16[288,3584]{1,0:T(8,128)(2,1)S(1)} %bitcast.10, bf16[288,3584]{1,0:T(8,128)(2,1)S(1)} %bitcast.12, bf16[288,3584]{1,0:T(8,128)(2,1)} %collective-permute-done.2.refs_3_, bf16[288,3584]{1,0:T(8,128)(2,1)} %collective-permute-done.3.refs_4_, ...), custom_call_target="tpu_custom_call" | custom-call | flops 1585446912 | bytes 14221312 | tf_op jit(solution)/shard_map/feed/pallas_call | solution.py:237
  102.8 17.6 %all_to_all.35 = bf16[16,8,3584]{2,1,0:T(8,128)(2,1)S(1)} all-to-all(bf16[16,8,3584]{2,1,0:T(8,128)(2,1)S(1)} %bitcast.8), channel_id=1, replica_groups={{0,16,32,48,64,80,96,112,128,144,160,176,192,208,224,240},{8,24,40,56,7..., dimensions={0} | all-to-all | bytes 1835008 | tf_op jit(solution)/shard_map/all_to_all | solution.py:262
  120.3 0.1 convert_reduce_fusion
  120.4 0.6 add_convert_fusion
  (30 shorter events, 0.2 us)
Async XLA Ops:
  0.0 46.0 %collective-permute-start.1 = (bf16[512,3584]{1,0:T(8,128)(2,1)}, bf16[512,3584]{1,0:T(8,128)(2,1)}, u32[]{:S(2)}, u32[]{:S(2)}) collective-permute-start(bf16[512,3584]{1,0:T(8,128)(2,1)} %refs_4_.3), channel_id=1, source_target_pairs={{0,8},{8,0},{16,24},{24,16},{32,40},{40,32},{48,56},{56,48},{64,72... | collective-permute-start | bytes 11010056 | tf_op jit(solution)/shard_map/ppermute | solution.py:259
  0.7 1.9 %copy-start.1 = (bf16[8,384,512]{2,1,0:T(8,128)(2,1)S(1)}, bf16[8,384,512]{2,1,0:T(8,128)(2,1)}, u32[]{:S(2)}) copy-start(bf16[8,384,512]{2,1,0:T(8,128)(2,1)} %refs_6_.1) | copy-start | bytes 9437188
  2.5 1.2 %copy-start.5 = (bf16[8,128,512]{2,1,0:T(8,128)(2,1)S(1)}, bf16[8,128,512]{2,1,0:T(8,128)(2,1)}, u32[]{:S(2)}) copy-start(bf16[8,128,512]{2,1,0:T(8,128)(2,1)} %refs_4_.2) | copy-start | bytes 3145732
  3.8 1.0 copy-start.10
  4.8 0.9 copy-start.11
  5.7 0.7 copy-start.12
  6.4 0.7 copy-start.13
  7.1 0.7 copy-start.14
  20.3 7.2 %copy-start.6 = (bf16[4,512,128]{2,1,0:T(8,128)(2,1)S(1)}, bf16[4,512,128]{2,1,0:T(8,128)(2,1)}, u32[]{:S(2)}) copy-start(bf16[4,512,128]{2,1,0:T(8,128)(2,1)} %refs_2_.3) | copy-start | bytes 1572868
  20.3 25.7 %all-to-all-start = ((bf16[16,64,512]{2,1,0:T(8,128)(2,1)}), bf16[16,64,512]{2,1,0:T(8,128)(2,1)S(1)}, u32[]{:S(2)}, u32[]{:S(2)}) async-start(bf16[16,64,512]{2,1,0:T(8,128)(2,1)} %bitcast.1), calls=%async_computation | async-start | bytes 2097152 | tf_op jit(solution)/shard_map/all_to_all | solution.py:262
  27.5 2.0 %collective-permute-start = (bf16[4,512,128]{2,1,0:T(8,128)(2,1)S(1)}, bf16[4,512,128]{2,1,0:T(8,128)(2,1)S(1)}, u32[]{:S(2)}, u32[]{:S(2)}) collective-permute-start(bf16[4,512,128]{2,1,0:T(8,128)(2,1)S(1)} %copy-done.6), channel_id=1, source_target_pairs={{0,8},{8,0},{16,24},{24,16},{32,40},{40,32},{48,56},{56,48},{64,72... | collective-permute-start | bytes 1572872 | tf_op jit(solution)/shard_map/ppermute | solution.py:259
  29.5 0.8 copy-start.8
  46.0 2.0 %copy-start = (bf16[512,3584]{1,0:T(8,128)(2,1)S(1)}, bf16[512,3584]{1,0:T(8,128)(2,1)}, u32[]{:S(2)}) copy-start(bf16[512,3584]{1,0:T(8,128)(2,1)} %refs_4_.3) | copy-start | bytes 11010052
  48.0 1.0 copy-start.7
  49.0 1.0 copy-start.9
  50.1 8.4 %copy-start.2 = (bf16[3584,288]{0,1:T(8,128)(2,1)S(1)}, bf16[3584,288]{0,1:T(8,128)(2,1)}, u32[]{:S(2)}) copy-start(bf16[3584,288]{0,1:T(8,128)(2,1)} %param.27) | copy-start | bytes 6193156
  50.1 9.1 %copy-start.16 = (bf16[3584]{0:T(1024)(128)(2,1)S(1)}, bf16[3584]{0:T(1024)(128)(2,1)}, u32[]{:S(2)}) copy-start(bf16[3584]{0:T(1024)(128)(2,1)} %param.26) | copy-start | bytes 21508
  54.7 18.8 %copy-start.15 = (bf16[8,3584]{1,0:T(8,128)(2,1)S(1)}, bf16[8,3584]{1,0:T(8,128)(2,1)}, u32[]{:S(2)}) copy-start(bf16[8,3584]{1,0:T(8,128)(2,1)} %param.15) | copy-start | bytes 172036
  54.7 18.7 %all-to-all-start.1 = ((bf16[16,8,3584]{2,1,0:T(8,128)(2,1)}), bf16[16,8,3584]{2,1,0:T(8,128)(2,1)S(1)}, u32[]{:S(2)}, u32[]{:S(2)}) async-start(bf16[16,8,3584]{2,1,0:T(8,128)(2,1)} %bitcast.2), calls=%async_computation.1 | async-start | bytes 1835008 | tf_op jit(solution)/shard_map/all_to_all | solution.py:262
  58.5 20.1 %collective-permute-start.2 = (bf16[288,3584]{1,0:T(8,128)(2,1)S(1)}, bf16[288,3584]{1,0:T(8,128)(2,1)}, u32[]{:S(2)}, u32[]{:S(2)}) collective-permute-start(bf16[288,3584]{1,0:T(8,128)(2,1)S(1)} %bitcast.9), channel_id=1, source_target_pairs={{0,8},{8,0},{16,24},{24,16},{32,40},{40,32},{48,56},{56,48},{64,72... | collective-permute-start | bytes 6193160 | tf_op jit(solution)/shard_map/ppermute | solution.py:259
  58.6 20.0 %collective-permute-start.3 = (bf16[288,3584]{1,0:T(8,128)(2,1)}, bf16[288,3584]{1,0:T(8,128)(2,1)}, u32[]{:S(2)}, u32[]{:S(2)}) collective-permute-start(bf16[288,3584]{1,0:T(8,128)(2,1)} %bitcast.11), channel_id=1, source_target_pairs={{0,8},{8,0},{16,24},{24,16},{32,40},{40,32},{48,56},{56,48},{64,72... | collective-permute-start | bytes 6193160 | tf_op jit(solution)/shard_map/ppermute | solution.py:259
  59.1 19.5 %collective-permute-start.4 = (bf16[288,3584]{1,0:T(8,128)(2,1)}, bf16[288,3584]{1,0:T(8,128)(2,1)}, u32[]{:S(2)}, u32[]{:S(2)}) collective-permute-start(bf16[288,3584]{1,0:T(8,128)(2,1)} %refs_5_.3), channel_id=1, source_target_pairs={{0,8},{8,0},{16,24},{24,16},{32,40},{40,32},{48,56},{56,48},{64,72... | collective-permute-start | bytes 6193160 | tf_op jit(solution)/shard_map/ppermute | solution.py:259
  74.8 17.8 %all-to-all-start.2 = ((bf16[16,8,3584]{2,1,0:T(8,128)(2,1)}), bf16[16,8,3584]{2,1,0:T(8,128)(2,1)S(1)}, u32[]{:S(2)}, u32[]{:S(2)}) async-start(bf16[16,8,3584]{2,1,0:T(8,128)(2,1)} %broadcast_in_dim.2), calls=%async_computation.2 | async-start | bytes 1835008 | tf_op jit(solution)/shard_map/all_to_all | solution.py:262
  92.6 1.6 %copy-start.3 = (bf16[3584,288]{0,1:T(8,128)(2,1)S(1)}, bf16[3584,288]{0,1:T(8,128)(2,1)}, u32[]{:S(2)}) copy-start(bf16[3584,288]{0,1:T(8,128)(2,1)} %param.28) | copy-start | bytes 6193156
  94.2 1.6 %copy-start.4 = (bf16[288,3584]{1,0:T(8,128)(2,1)S(1)}, bf16[288,3584]{1,0:T(8,128)(2,1)}, u32[]{:S(2)}) copy-start(bf16[288,3584]{1,0:T(8,128)(2,1)} %refs_5_.3) | copy-start | bytes 6193156

commit v3 on v2

v3 whole, which is shorter than its diff:
```python
import jax
import jax.numpy as jnp
from jax import lax
from jax.experimental import pallas as pl
from jax.experimental.pallas import tpu as pltpu
from jax.sharding import PartitionSpec as P

F32, BF16 = jnp.float32, jnp.bfloat16
VMEM_BYTES = 60 * 2**20
IN_FLIGHT = 8
ROOMY_BYTES = 52 * 2**20
HBM = pl.BlockSpec(memory_space=pltpu.HBM)
VMEM = pl.BlockSpec(memory_space=pltpu.VMEM)
SMEM = pl.BlockSpec(memory_space=pltpu.SMEM)


def normalize(values, gain):
    scaled = values * lax.rsqrt(jnp.mean(values * values, axis=-1, keepdims=True) + 1e-06)
    return (scaled * gain.astype(F32)).astype(BF16)


def mul(a, b, a_dim=1, b_dim=0):
    return lax.dot_general(a, b, (((a_dim,), (b_dim,)), ((), ())), preferred_element_type=F32)


def cost(flops, size):
    return pl.CostEstimate(flops=flops, bytes_accessed=size, transcendentals=0)


class Stream:
    def __init__(self, copies, window):
        self.copies, self.started, self.done = copies, 0, 0
        self.window = window
        self.fill()

    def fill(self):
        while self.started < min(len(self.copies), self.done + self.window):
            self.copies[self.started].start()
            self.started += 1

    def need(self, count):
        while self.done < count:
            self.copies[self.done].wait()
            self.done += 1
            self.fill()


def attend_kernel(
    scale,
    lengths_hbm,
    counts_hbm,
    new_latent_hbm,
    new_rope_hbm,
    q_latent_hbm,
    q_rope_hbm,
    cache_latent_hbm,
    cache_rope_hbm,
    out_ref,
    lengths,
    counts,
    n_lat,
    n_rot,
    q_lat,
    q_rot,
    c_lat,
    c_rot,
    scores,
    acc,
    sems,
):
    rows, heads, width = q_lat.shape
    positions = c_lat.shape[1]
    step = 2
    whole = (
        (lengths_hbm, lengths),
        (counts_hbm, counts),
        (new_latent_hbm, n_lat),
        (new_rope_hbm, n_rot),
        (q_rope_hbm, q_rot),
        (cache_rope_hbm, c_rot),
    )
    copies = [pltpu.make_async_copy(src, dst, sems.at[i]) for i, (src, dst) in enumerate(whole)]
    for g in range(rows // step):
        at = pl.ds(g * step, step)
        for src, dst in ((q_latent_hbm, q_lat), (cache_latent_hbm, c_lat)):
            copies.append(pltpu.make_async_copy(src.at[at], dst.at[at], sems.at[len(copies)]))
    stream = Stream(copies, len(whole) + 4)
    stream.need(len(whole))
    position = lax.broadcasted_iota(jnp.int32, (heads, positions), 1)
    fresh_lat = n_lat[...]
    fresh_rot = n_rot[...]
    fresh = []
    for t in range(rows):
        stream.need(len(whole) + 2 * (t // step + 1))
        used = jnp.where(t < counts[0], lengths[t], 0)
        q = q_lat[t]
        rot = q_rot[t].T
        part = (mul(q, c_lat[t], 1, 1) + mul(rot, c_rot[t])) * scale
        scores[t] = jnp.where(position < used, part, -jnp.inf)
        both = (mul(q, fresh_lat, 1, 1) + mul(rot, fresh_rot, 1, 1)) * scale
        fresh.append(both[:, t : t + 1])
    for t in range(rows):
        part = scores[t]
        top = jnp.maximum(jnp.max(part, axis=1, keepdims=True), fresh[t])
        expo = jnp.exp(part - top)
        fresh_expo = jnp.exp(fresh[t] - top)
        inverse = 1.0 / (jnp.sum(expo, axis=1, keepdims=True) + fresh_expo)
        probs = (expo * inverse).astype(BF16)
        fresh_prob = (fresh_expo * inverse).astype(BF16).astype(F32)
        o = mul(probs, c_lat[t]) + fresh_prob * fresh_lat[t : t + 1].astype(F32)
        for j in range(width // 128):
            acc[j, pl.ds(t, heads, stride=rows), :] = o[:, j * 128 : (j + 1) * 128]
    for j in range(width // 128):
        out_ref[:, j * 128 : (j + 1) * 128] = acc[j].astype(BF16)


def attend(scale, q_latent, q_rope, cache_latent, cache_rope, new_latent, new_rope, lengths, counts):
    rows, heads, width = q_latent.shape
    positions = cache_latent.shape[1]

    def body(*refs):
        attend_kernel(scale, *refs)

    size = 2 * (q_latent.size * 2 + cache_latent.size + q_rope.size + cache_rope.size)
    flops = 4 * rows * heads * positions * width
    return pl.pallas_call(
        body,
        out_shape=jax.ShapeDtypeStruct((heads * rows, width), BF16),
        in_specs=[HBM] * 8,
        out_specs=VMEM,
        scratch_shapes=[
            pltpu.SMEM(lengths.shape, jnp.int32),
            pltpu.SMEM(counts.shape, jnp.int32),
            pltpu.VMEM(new_latent.shape, BF16),
            pltpu.VMEM(new_rope.shape, BF16),
            pltpu.VMEM(q_latent.shape, BF16),
            pltpu.VMEM(q_rope.shape, BF16),
            pltpu.VMEM(cache_latent.shape, BF16),
            pltpu.VMEM(cache_rope.shape, BF16),
            pltpu.VMEM((rows, heads, positions), F32),
            pltpu.VMEM((width // 128, heads * rows, 128), F32),
            pltpu.SemaphoreType.DMA((6 + rows,)),
        ],
        compiler_params=pltpu.CompilerParams(vmem_limit_bytes=VMEM_BYTES),
        cost_estimate=cost(flops, size),
        name="attend",
    )(lengths, counts, new_latent, new_rope, q_latent, q_rope, cache_latent, cache_rope)


def send_out(out, out_hbm, n, block, sems, base):
    at = pl.ds(n * block, block)
    leave = pltpu.make_async_copy(out.at[:, at], out_hbm.at[:, at], sems.at[base + n])
    leave.start()
    return leave


def project_kernel(
    block, core_ref, got_hbm, uv1_hbm, uv2_hbm, wo1_hbm, wo2_hbm, out_hbm, got, uv, wo, heads_v, out, sems
):
    chips, span, width = got.shape
    heads, _, hv = uv1_hbm.shape
    rows = span // (2 * heads)
    depth, cols = wo1_hbm.shape
    copies = [pltpu.make_async_copy(got_hbm, got, sems.at[0])]
    for i, src in enumerate((uv1_hbm, uv2_hbm)):
        to = uv.at[pl.ds(i * heads, heads)]
        copies.append(pltpu.make_async_copy(src, to, sems.at[len(copies)]))
    for n in range(cols // block):
        at = pl.ds(n * block, block)
        for i, src in enumerate((wo1_hbm, wo2_hbm)):
            to = wo.at[pl.ds(i * depth, depth), at]
            copies.append(pltpu.make_async_copy(src.at[:, at], to, sems.at[len(copies)]))
    stream = Stream(copies, IN_FLIGHT + 3)
    stream.need(1)
    core = core_ref[0]
    half = heads * rows
    for s in range(2):
        which = core if s == 0 else 1 - core
        mine = got[:, pl.ds(pl.multiple_of(which * half, half), half), :].astype(F32)
        stream.need(s + 2)
        for i in range(heads):
            x = mine[:, i * rows : (i + 1) * rows, :].reshape(chips * rows, width).astype(BF16)
            n = s * heads + i
            heads_v[:, n * hv : (n + 1) * hv] = mul(x, uv[n]).astype(BF16)
    x = heads_v[...]
    leaving = []
    for n in range(cols // block):
        stream.need(3 + 2 * (n + 1))
        at = slice(n * block, (n + 1) * block)
        out[:, at] = mul(x, wo[:, at]).astype(BF16)
        leaving.append(send_out(out, out_hbm, n, block, sems, len(copies)))
    for c in leaving:
        c.wait()


def project(core, got, w_uv, w_uv2, w_o, w_o2):
    chips, span, width = got.shape
    heads, _, hv = w_uv.shape
    rows = chips * span // (2 * heads)
    depth, cols = w_o.shape
    block = 512

    def body(*refs):
        project_kernel(block, *refs)

    size = 2 * (got.size + 2 * w_uv.size + 2 * w_o.size + rows * cols)
    return pl.pallas_call(
        body,
        out_shape=jax.ShapeDtypeStruct((rows, cols), BF16),
        in_specs=[SMEM, HBM, HBM, HBM, HBM, HBM],
        out_specs=HBM,
        scratch_shapes=[
            pltpu.VMEM(got.shape, BF16),
            pltpu.VMEM((2 * heads, width, hv), BF16),
            pltpu.VMEM((2 * depth, cols), BF16),
            pltpu.VMEM((rows, 2 * depth), BF16),
            pltpu.VMEM((rows, cols), BF16),
            pltpu.SemaphoreType.DMA((3 + 3 * (cols // block),)),
        ],
        compiler_params=pltpu.CompilerParams(vmem_limit_bytes=ROOMY_BYTES),
        cost_estimate=cost(4 * rows * w_o.size, size),
        name="project",
    )(core, got, w_uv, w_uv2, w_o, w_o2)


def spans(first, size, total):
    edges = [0] + list(range(first, total, size)) + [total]
    return list(zip(edges[:-1], edges[1:]))


def feed_kernel(
    pieces, piece, block, x_ref, gate1, up1, gate2, up2, down1, down2, out_ref, gate_w, up_w, down_w, act, sems
):
    hidden, width = gate1.shape
    count = 0

    def copy(src, dst, rows, to, cols):
        nonlocal count
        count += 1
        return pltpu.make_async_copy(
            src.at[rows, cols], dst.at[to, cols], sems.at[count - 1]
        )

    everything = pl.ds(0, width)
    copies, ready = [], []
    for lo, hi in pieces:
        for dst, pair in ((gate_w, (gate1, gate2)), (up_w, (up1, up2))):
            for core, src in enumerate(pair):
                a, b = max(lo, core * hidden), min(hi, (core + 1) * hidden)
                for c in range(a, b, piece):
                    size = min(piece, b - c)
                    rows = pl.ds(c - core * hidden, size)
                    copies.append(copy(src, dst, rows, pl.ds(c, size), everything))
        ready.append(len(copies))
    for n in range(width // block):
        cols = pl.ds(n * block, block)
        for core, src in enumerate((down1, down2)):
            rows, to = pl.ds(0, hidden), pl.ds(core * hidden, hidden)
            copies.append(copy(src, down_w, rows, to, cols))
    stream = Stream(copies, IN_FLIGHT)
    x = x_ref[...]
    for (lo, hi), count in zip(pieces, ready):
        stream.need(count)
        gate = mul(x, gate_w[lo:hi], 1, 1)
        upper = mul(x, up_w[lo:hi], 1, 1)
        act[:, lo:hi] = (gate / (1.0 + jnp.exp(-gate)) * upper).astype(BF16)
    activated = act[...]
    for n in range(width // block):
        stream.need(ready[-1] + 2 * (n + 1))
        at = slice(n * block, (n + 1) * block)
        out_ref[:, at] = mul(activated, down_w[:, at]).astype(BF16)


def feed(x, *weights):
    rows, width = x.shape
    hidden = weights[0].shape[0]
    block = 512
    pieces = spans(256, 256, 2 * hidden)

    def body(*refs):
        feed_kernel(pieces, 96, block, *refs)

    size = 2 * (2 * x.size + sum(w.size for w in weights))
    return pl.pallas_call(
        body,
        out_shape=jax.ShapeDtypeStruct((rows, width), BF16),
        in_specs=[VMEM] + [HBM] * 6,
        out_specs=VMEM,
        scratch_shapes=[pltpu.VMEM((2 * hidden, width), BF16)] * 3
        + [
            pltpu.VMEM((rows, 2 * hidden), BF16),
            pltpu.SemaphoreType.DMA((48,)),
        ],
        compiler_params=pltpu.CompilerParams(vmem_limit_bytes=ROOMY_BYTES),
        cost_estimate=cost(12 * rows * weights[0].size, size),
        name="feed",
    )(x, *weights)


def solution(mesh):
    n_dp = mesh.shape["dp"]
    chips = n_dp // 2
    swap = [(i, i ^ 1) for i in range(n_dp)]
    same_core = [[2 * c + k for c in range(chips)] for k in range(2)]

    def sibling(w):
        return lax.ppermute(w, "dp", swap)

    def exchange(v):
        return lax.all_to_all(v, "dp", 0, 0, axis_index_groups=same_core, tiled=True)

    def summed(part, rows):
        got = exchange(part).reshape(chips, rows, part.shape[-1])
        return jnp.sum(got.astype(F32), axis=0)

    def on_device(
        residual_in,
        q_latent,
        q_rope,
        cache_latent,
        cache_rope,
        new_latent,
        new_rope,
        lengths,
        counts,
        w_uv,
        w_o,
        norm_gain,
        w_gate,
        w_up,
        w_down,
    ):
        rows = residual_in.shape[0]
        core = (lax.axis_index("dp") & 1).astype(jnp.int32).reshape(1)
        gate_t, up_t = w_gate.T, w_up.T
        w_uv2, w_o2 = sibling(w_uv), sibling(w_o)
        gate2, up2, down2 = sibling(gate_t), sibling(up_t), sibling(w_down)
        scale = (w_uv.shape[2] + q_rope.shape[1]) ** (-0.5)
        o_latent = attend(
            scale, q_latent, q_rope, cache_latent, cache_rope, new_latent, new_rope, lengths, counts
        )
        got = exchange(o_latent).reshape(chips, -1, o_latent.shape[1])
        part = project(core, got, w_uv, w_uv2, w_o, w_o2)
        hidden_mine = residual_in.astype(F32) + summed(part, rows)
        normed_mine = normalize(hidden_mine, norm_gain)
        copies = jnp.broadcast_to(normed_mine[None], (chips,) + normed_mine.shape)
        normed = exchange(copies.reshape(chips * rows, -1))
        part = feed(normed, gate_t, up_t, gate2, up2, w_down, down2)
        return (hidden_mine + summed(part, rows)).astype(BF16)

    placed = (
        P(("rep", "dp"), None),
        P(("rep", "dp"), None, None),
        P(("rep", "dp"), None, None),
        P(("rep", "dp"), None, None),
        P(("rep", "dp"), None, None),
        P(("rep", "dp"), None),
        P(("rep", "dp"), None),
        P(("rep", "dp")),
        P(("rep", "dp")),
        P("dp", None, None),
        P("dp", None),
        P(),
        P(None, "dp"),
        P(None, "dp"),
        P("dp", None),
    )
    return jax.shard_map(
        on_device, mesh=mesh, in_specs=placed, out_specs=P(("rep", "dp"), None), check_vma=False
    )
```

time: 122 us -> 104 us (0.85)
  local copies, waits for them, and re-layouts: 16.1 us -> 2.01 us
  Pallas kernels: 24.2 us -> 20 us
    unnamed x34 -> x10, local copies, waits for them, and re-layouts: 15.1 us -> 1.01 us
    pallas_call x1, Pallas kernels: 12.6 us -> 7.21 us  [attend(): pl.pallas_call(body, out_shape=jax.ShapeDtypeStruct((heads * rows, width)...]
  transfers between devices with their start and end apart: 8 -> 8, of which waited for: 4 -> 4; matrix products, arithmetic and copies ran while one was open for 1% -> 1% of each run, Pallas kernels for 10% -> 7%
where the time goes in v3:
time: 104 us; the launch traced here: 103 us
  waiting for transfers between devices  46.4 us (45%)
  Pallas kernels  20 us (19%)
  blocking collectives  17.5 us (17%)
  starting transfers between devices  15.6 us (15%)
  local copies, waits for them, and re-layouts  2.01 us (2%)
  other arithmetic  1.13 us (1%)
    all_to_all x3, waiting for transfers between devices, exchange(): lax.all_to_all(v, 'dp', 0, 0, axis_index_groups=same_core, tiled=True)  44.7 us
    all_to_all x1, blocking collectives, exchange(): lax.all_to_all(v, 'dp', 0, 0, axis_index_groups=same_core, tiled=True)  17.5 us
    all_to_all x3, starting transfers between devices, exchange(): lax.all_to_all(v, 'dp', 0, 0, axis_index_groups=same_core, tiled=True)  14.6 us
    pallas_call x1, Pallas kernels, feed(): pl.pallas_call(body, out_shape=jax.ShapeDtypeStruct((rows, width), BF16),...  7.73 us
    pallas_call x1, Pallas kernels, attend(): pl.pallas_call(body, out_shape=jax.ShapeDtypeStruct((heads * rows, width)...  7.21 us
    pallas_call x1, Pallas kernels, project(): pl.pallas_call(body, out_shape=jax.ShapeDtypeStruct((rows, cols), BF16),...  5.01 us
  transfers between devices with their start and end apart: 8, of which 4 were waited for; matrix products, arithmetic and copies ran while one was open for 1% of the time, Pallas kernels for 7%

profile of v3, /device:TPU:192, one launch (start us, length us, event | category | flops | bytes accessed | tf_op | source)
XLA Modules:
  0.0 103.5 jit_solution(5746270726777849494)
XLA Ops:
  0.0 0.0 collective-permute-start.1
  0.7 7.2 %attend.1 = bf16[1024,512]{1,0:T(8,128)(2,1)} custom-call(s32[8]{0:T(128)} %refs_0_.1, s32[1]{0:T(128)S(6)} %copy.16.refs_1_, bf16[8,512]{1,0:T(8,128)(2,1)} %refs_2_.2, bf16[8,64]{1,0:T(8,128)(2,1)} %refs_3_.1, bf16[8,128,512]{2,1,0:T(8,128)(2,1)} %refs_4_.2, bf16[8,64,128]{2,1,0:T(8,128)(2,1)} %refs_5_.2, bf16[8,384,512]{2,1,0:T(8,128)(2,1)} %refs_6_.1, ...), custom_call_target="tpu_custom_call" | custom-call | flops 805306368 | bytes 5767168 | tf_op jit(solution)/shard_map/attend/pallas_call | solution.py:126
  7.9 0.0 copy-start
  7.9 7.2 %all-to-all-start = ((bf16[16,64,512]{2,1,0:T(8,128)(2,1)}), bf16[16,64,512]{2,1,0:T(8,128)(2,1)S(1)}, u32[]{:S(2)}, u32[]{:S(2)}) async-start(bf16[16,64,512]{2,1,0:T(8,128)(2,1)} %bitcast.9), calls=%async_computation | async-start | bytes 2097152 | tf_op jit(solution)/shard_map/all_to_all | solution.py:310
  15.1 0.0 copy-done
  15.1 0.3 collective-permute-start
  15.4 1.7 %collective-permute-done.refs_3_ = bf16[4,512,128]{2,1,0:T(8,128)(2,1)S(1)} collective-permute-done((bf16[4,512,128]{2,1,0:T(8,128)(2,1)S(1)}, bf16[4,512,128]{2,1,0:T(8,128)(2,1)S(1)}, u32[]{:S(2)}, u32[]{:S(2)}) %collective-permute-start) | collective-permute-done | bytes 524320 | tf_op jit(solution)/shard_map/ppermute | solution.py:307
  17.1 16.5 %all-to-all-done.refs_1_ = bf16[16,64,512]{2,1,0:T(8,128)(2,1)S(1)} async-done(((bf16[16,64,512]{2,1,0:T(8,128)(2,1)}), bf16[16,64,512]{2,1,0:T(8,128)(2,1)S(1)}, u32[]{:S(2)}, u32[]{:S(2)}) %all-to-all-start) | async-done | bytes 1048608 | tf_op jit(solution)/shard_map/all_to_all | solution.py:310
  33.6 0.0 collective-permute-done.1.refs_5_
  33.6 1.0 copy-done.1
  34.5 5.0 %project.1 = bf16[128,3584]{1,0:T(8,128)(2,1)} custom-call(s32[1]{0:T(128)} %bitcast.refs_0_, bf16[16,64,512]{2,1,0:T(8,128)(2,1)} %copy-done.1, bf16[4,512,128]{2,1,0:T(8,128)(2,1)S(1)} %copy-done, bf16[4,512,128]{2,1,0:T(8,128)(2,1)S(1)} %collective-permute-done.refs_3_, bf16[512,3584]{1,0:T(8,128)(2,1)} %refs_4_.3, ...), custom_call_target="tpu_custom_call" | custom-call | flops 939524096 | bytes 10354688 | tf_op jit(solution)/shard_map/project/pallas_call | solution.py:207
  39.6 0.0 copy-start.3
  39.6 3.8 %all-to-all-start.1 = ((bf16[16,8,3584]{2,1,0:T(8,128)(2,1)}), bf16[16,8,3584]{2,1,0:T(8,128)(2,1)S(1)}, u32[]{:S(2)}, u32[]{:S(2)}) async-start(bf16[16,8,3584]{2,1,0:T(8,128)(2,1)} %bitcast.2), calls=%async_computation.1 | async-start | bytes 1835008 | tf_op jit(solution)/shard_map/all_to_all | solution.py:310
  43.4 0.1 collective-permute-start.2
  43.5 0.5 collective-permute-start.3
  44.0 0.1 collective-permute-start.4
  44.1 0.0 copy-done.4
  44.1 14.2 %all-to-all-done.1 = bf16[16,8,3584]{2,1,0:T(8,128)(2,1)S(1)} async-done(((bf16[16,8,3584]{2,1,0:T(8,128)(2,1)}), bf16[16,8,3584]{2,1,0:T(8,128)(2,1)S(1)}, u32[]{:S(2)}, u32[]{:S(2)}) %all-to-all-start.1) | async-done | bytes 917536 | tf_op jit(solution)/shard_map/all_to_all | solution.py:310
  58.2 0.1 convert_reduce_fusion.1
  58.4 0.0 copy-done.3
  58.4 0.1 multiply_reduce_fusion
  58.5 0.1 multiply_convert_fusion
  58.6 1.0 broadcast_in_dim.2
  59.6 3.6 %all-to-all-start.2 = ((bf16[16,8,3584]{2,1,0:T(8,128)(2,1)}), bf16[16,8,3584]{2,1,0:T(8,128)(2,1)S(1)}, u32[]{:S(2)}, u32[]{:S(2)}) async-start(bf16[16,8,3584]{2,1,0:T(8,128)(2,1)} %broadcast_in_dim.2), calls=%async_computation.2 | async-start | bytes 1835008 | tf_op jit(solution)/shard_map/all_to_all | solution.py:310
  63.3 0.0 collective-permute-done.2.refs_3_
  63.3 0.0 collective-permute-done.3.refs_4_
  63.3 0.0 collective-permute-done.4.refs_6_
  63.3 14.1 %all-to-all-done.2 = bf16[16,8,3584]{2,1,0:T(8,128)(2,1)S(1)} async-done(((bf16[16,8,3584]{2,1,0:T(8,128)(2,1)}), bf16[16,8,3584]{2,1,0:T(8,128)(2,1)S(1)}, u32[]{:S(2)}, u32[]{:S(2)}) %all-to-all-start.2) | async-done | bytes 917536 | tf_op jit(solution)/shard_map/all_to_all | solution.py:310
  77.4 7.7 %feed.1 = bf16[128,3584]{1,0:T(8,128)(2,1)S(1)} custom-call(bf16[128,3584]{1,0:T(8,128)(2,1)S(1)} %bitcast.7, bf16[288,3584]{1,0:T(8,128)(2,1)} %bitcast.11, bf16[288,3584]{1,0:T(8,128)(2,1)} %bitcast.13, bf16[288,3584]{1,0:T(8,128)(2,1)} %copy-done.2, bf16[288,3584]{1,0:T(8,128)(2,1)} %collective-permute-done.3.refs_4_, bf16[288,3584]{1,0:T(8,128)(2,1)} %refs_5_.3, ...), custom_call_target="tpu_custom_call" | custom-call | flops 1585446912 | bytes 14221312 | tf_op jit(solution)/shard_map/feed/pallas_call | solution.py:284
  85.2 17.5 %all_to_all.35 = bf16[16,8,3584]{2,1,0:T(8,128)(2,1)S(1)} all-to-all(bf16[16,8,3584]{2,1,0:T(8,128)(2,1)S(1)} %bitcast.8), channel_id=1, replica_groups={{0,16,32,48,64,80,96,112,128,144,160,176,192,208,224,240},{8,24,40,56,7..., dimensions={0} | all-to-all | bytes 1835008 | tf_op jit(solution)/shard_map/all_to_all | solution.py:310
  102.7 0.1 convert_reduce_fusion
  102.8 0.6 add_convert_fusion
  (6 shorter events, 0.0 us)
Async XLA Ops:
  0.0 33.6 %collective-permute-start.1 = (bf16[512,3584]{1,0:T(8,128)(2,1)}, bf16[512,3584]{1,0:T(8,128)(2,1)}, u32[]{:S(2)}, u32[]{:S(2)}) collective-permute-start(bf16[512,3584]{1,0:T(8,128)(2,1)} %refs_4_.3), channel_id=1, source_target_pairs={{0,8},{8,0},{16,24},{24,16},{32,40},{40,32},{48,56},{56,48},{64,72... | collective-permute-start | bytes 11010056 | tf_op jit(solution)/shard_map/ppermute | solution.py:307
  7.9 7.2 %copy-start = (bf16[4,512,128]{2,1,0:T(8,128)(2,1)S(1)}, bf16[4,512,128]{2,1,0:T(8,128)(2,1)}, u32[]{:S(2)}) copy-start(bf16[4,512,128]{2,1,0:T(8,128)(2,1)} %refs_2_.3) | copy-start | bytes 1572868
  7.9 25.7 %all-to-all-start = ((bf16[16,64,512]{2,1,0:T(8,128)(2,1)}), bf16[16,64,512]{2,1,0:T(8,128)(2,1)S(1)}, u32[]{:S(2)}, u32[]{:S(2)}) async-start(bf16[16,64,512]{2,1,0:T(8,128)(2,1)} %bitcast.9), calls=%async_computation | async-start | bytes 2097152 | tf_op jit(solution)/shard_map/all_to_all | solution.py:310
  15.1 2.0 %collective-permute-start = (bf16[4,512,128]{2,1,0:T(8,128)(2,1)S(1)}, bf16[4,512,128]{2,1,0:T(8,128)(2,1)S(1)}, u32[]{:S(2)}, u32[]{:S(2)}) collective-permute-start(bf16[4,512,128]{2,1,0:T(8,128)(2,1)S(1)} %copy-done), channel_id=1, source_target_pairs={{0,8},{8,0},{16,24},{24,16},{32,40},{40,32},{48,56},{56,48},{64,72... | collective-permute-start | bytes 1572872 | tf_op jit(solution)/shard_map/ppermute | solution.py:307
  33.5 1.0 copy-start.1
  34.5 9.5 %copy-start.4 = (bf16[3584]{0:T(1024)(128)(2,1)S(1)}, bf16[3584]{0:T(1024)(128)(2,1)}, u32[]{:S(2)}) copy-start(bf16[3584]{0:T(1024)(128)(2,1)} %param.26) | copy-start | bytes 21508
  39.6 18.8 %copy-start.3 = (bf16[8,3584]{1,0:T(8,128)(2,1)S(1)}, bf16[8,3584]{1,0:T(8,128)(2,1)}, u32[]{:S(2)}) copy-start(bf16[8,3584]{1,0:T(8,128)(2,1)} %param.15) | copy-start | bytes 172036
  39.6 18.7 %all-to-all-start.1 = ((bf16[16,8,3584]{2,1,0:T(8,128)(2,1)}), bf16[16,8,3584]{2,1,0:T(8,128)(2,1)S(1)}, u32[]{:S(2)}, u32[]{:S(2)}) async-start(bf16[16,8,3584]{2,1,0:T(8,128)(2,1)} %bitcast.2), calls=%async_computation.1 | async-start | bytes 1835008 | tf_op jit(solution)/shard_map/all_to_all | solution.py:310
  43.4 19.9 %collective-permute-start.2 = (bf16[288,3584]{1,0:T(8,128)(2,1)}, bf16[288,3584]{1,0:T(8,128)(2,1)S(1)}, u32[]{:S(2)}, u32[]{:S(2)}) collective-permute-start(bf16[288,3584]{1,0:T(8,128)(2,1)} %bitcast.10), channel_id=1, source_target_pairs={{0,8},{8,0},{16,24},{24,16},{32,40},{40,32},{48,56},{56,48},{64,72... | collective-permute-start | bytes 6193160 | tf_op jit(solution)/shard_map/ppermute | solution.py:307
  43.5 19.8 %collective-permute-start.3 = (bf16[288,3584]{1,0:T(8,128)(2,1)}, bf16[288,3584]{1,0:T(8,128)(2,1)}, u32[]{:S(2)}, u32[]{:S(2)}) collective-permute-start(bf16[288,3584]{1,0:T(8,128)(2,1)} %bitcast.12), channel_id=1, source_target_pairs={{0,8},{8,0},{16,24},{24,16},{32,40},{40,32},{48,56},{56,48},{64,72... | collective-permute-start | bytes 6193160 | tf_op jit(solution)/shard_map/ppermute | solution.py:307
  44.0 19.3 %collective-permute-start.4 = (bf16[288,3584]{1,0:T(8,128)(2,1)}, bf16[288,3584]{1,0:T(8,128)(2,1)}, u32[]{:S(2)}, u32[]{:S(2)}) collective-permute-start(bf16[288,3584]{1,0:T(8,128)(2,1)} %refs_5_.3), channel_id=1, source_target_pairs={{0,8},{8,0},{16,24},{24,16},{32,40},{40,32},{48,56},{56,48},{64,72... | collective-permute-start | bytes 6193160 | tf_op jit(solution)/shard_map/ppermute | solution.py:307
  59.6 17.8 %all-to-all-start.2 = ((bf16[16,8,3584]{2,1,0:T(8,128)(2,1)}), bf16[16,8,3584]{2,1,0:T(8,128)(2,1)S(1)}, u32[]{:S(2)}, u32[]{:S(2)}) async-start(bf16[16,8,3584]{2,1,0:T(8,128)(2,1)} %broadcast_in_dim.2), calls=%async_computation.2 | async-start | bytes 1835008 | tf_op jit(solution)/shard_map/all_to_all | solution.py:310
  63.3 14.1 %copy-start.2 = (bf16[288,3584]{1,0:T(8,128)(2,1)}, bf16[288,3584]{1,0:T(8,128)(2,1)S(1)}, u32[]{:S(2)}) copy-start(bf16[288,3584]{1,0:T(8,128)(2,1)S(1)} %collective-permute-done.2.refs_3_) | copy-start | bytes 6193156

commit v4 on v3

--- a/solution.py
+++ b/solution.py
@@ -7,7 +7,8 @@
 
 F32, BF16 = jnp.float32, jnp.bfloat16
 VMEM_BYTES = 60 * 2**20
-IN_FLIGHT = 8
+IN_FLIGHT = 12
+ATTEND_GROUPS = ((0, 2), (2, 8))
 ROOMY_BYTES = 52 * 2**20
 HBM = pl.BlockSpec(memory_space=pltpu.HBM)
 VMEM = pl.BlockSpec(memory_space=pltpu.VMEM)
@@ -43,6 +44,13 @@
             self.copies[self.done].wait()
             self.done += 1
             self.fill()
+
+
+def send_out(out, out_hbm, n, block, sems, base):
+    at = pl.ds(n * block, block)
+    leave = pltpu.make_async_copy(out.at[:, at], out_hbm.at[:, at], sems.at[base + n])
+    leave.start()
+    return leave
 
 
 def attend_kernel(
@@ -55,7 +63,7 @@
     q_rope_hbm,
     cache_latent_hbm,
     cache_rope_hbm,
-    out_ref,
+    out_hbm,
     lengths,
     counts,
     n_lat,
@@ -66,6 +74,7 @@
     c_rot,
     scores,
     acc,
+    out,
     sems,
 ):
     rows, heads, width = q_lat.shape
@@ -89,29 +98,35 @@
     position = lax.broadcasted_iota(jnp.int32, (heads, positions), 1)
     fresh_lat = n_lat[...]
     fresh_rot = n_rot[...]
-    fresh = []
-    for t in range(rows):
-        stream.need(len(whole) + 2 * (t // step + 1))
-        used = jnp.where(t < counts[0], lengths[t], 0)
-        q = q_lat[t]
-        rot = q_rot[t].T
-        part = (mul(q, c_lat[t], 1, 1) + mul(rot, c_rot[t])) * scale
-        scores[t] = jnp.where(position < used, part, -jnp.inf)
-        both = (mul(q, fresh_lat, 1, 1) + mul(rot, fresh_rot, 1, 1)) * scale
-        fresh.append(both[:, t : t + 1])
-    for t in range(rows):
-        part = scores[t]
-        top = jnp.maximum(jnp.max(part, axis=1, keepdims=True), fresh[t])
-        expo = jnp.exp(part - top)
-        fresh_expo = jnp.exp(fresh[t] - top)
-        inverse = 1.0 / (jnp.sum(expo, axis=1, keepdims=True) + fresh_expo)
-        probs = (expo * inverse).astype(BF16)
-        fresh_prob = (fresh_expo * inverse).astype(BF16).astype(F32)
-        o = mul(probs, c_lat[t]) + fresh_prob * fresh_lat[t : t + 1].astype(F32)
-        for j in range(width // 128):
-            acc[j, pl.ds(t, heads, stride=rows), :] = o[:, j * 128 : (j + 1) * 128]
+    for begin, end in ATTEND_GROUPS:
+        stream.need(len(whole) + 2 * (end // step))
+        fresh = []
+        for t in range(begin, end):
+            used = jnp.where(t < counts[0], lengths[t], 0)
+            q = q_lat[t]
+            rot = q_rot[t].T
+            part = (mul(q, c_lat[t], 1, 1) + mul(rot, c_rot[t])) * scale
+            scores[t] = jnp.where(position < used, part, -jnp.inf)
+            both = (mul(q, fresh_lat, 1, 1) + mul(rot, fresh_rot, 1, 1)) * scale
+            fresh.append(both[:, t : t + 1])
+        for t in range(begin, end):
+            part = scores[t]
+            new = fresh[t - begin]
+            top = jnp.maximum(jnp.max(part, axis=1, keepdims=True), new)
+            expo = jnp.exp(part - top)
+            fresh_expo = jnp.exp(new - top)
+            inverse = 1.0 / (jnp.sum(expo, axis=1, keepdims=True) + fresh_expo)
+            probs = (expo * inverse).astype(BF16)
+            fresh_prob = (fresh_expo * inverse).astype(BF16).astype(F32)
+            o = mul(probs, c_lat[t]) + fresh_prob * fresh_lat[t : t + 1].astype(F32)
+            for j in range(width // 128):
+                acc[j, pl.ds(t, heads, stride=rows), :] = o[:, j * 128 : (j + 1) * 128]
+    leaving = []
     for j in range(width // 128):
-        out_ref[:, j * 128 : (j + 1) * 128] = acc[j].astype(BF16)
+        out[:, j * 128 : (j + 1) * 128] = acc[j].astype(BF16)
+        leaving.append(send_out(out, out_hbm, j, 128, sems, len(copies)))
+    for c in leaving:
+        c.wait()
 
 
 def attend(scale, q_latent, q_rope, cache_latent, cache_rope, new_latent, new_rope, lengths, counts):
@@ -127,7 +142,7 @@
         body,
         out_shape=jax.ShapeDtypeStruct((heads * rows, width), BF16),
         in_specs=[HBM] * 8,
-        out_specs=VMEM,
+        out_specs=HBM,
         scratch_shapes=[
             pltpu.SMEM(lengths.shape, jnp.int32),
             pltpu.SMEM(counts.shape, jnp.int32),
@@ -139,19 +154,13 @@
             pltpu.VMEM(cache_rope.shape, BF16),
             pltpu.VMEM((rows, heads, positions), F32),
             pltpu.VMEM((width // 128, heads * rows, 128), F32),
-            pltpu.SemaphoreType.DMA((6 + rows,)),
+            pltpu.VMEM((heads * rows, width), BF16),
+            pltpu.SemaphoreType.DMA((6 + rows + width // 128,)),
         ],
         compiler_params=pltpu.CompilerParams(vmem_limit_bytes=VMEM_BYTES),
         cost_estimate=cost(flops, size),
         name="attend",
     )(lengths, counts, new_latent, new_rope, q_latent, q_rope, cache_latent, cache_rope)
-
-
-def send_out(out, out_hbm, n, block, sems, base):
-    at = pl.ds(n * block, block)
-    leave = pltpu.make_async_copy(out.at[:, at], out_hbm.at[:, at], sems.at[base + n])
-    leave.start()
-    return leave
 
 
 def project_kernel(
@@ -198,7 +207,7 @@
     heads, _, hv = w_uv.shape
     rows = chips * span // (2 * heads)
     depth, cols = w_o.shape
-    block = 512
+    block = 896
 
     def body(*refs):
         project_kernel(block, *refs)
@@ -275,7 +284,7 @@
     rows, width = x.shape
     hidden = weights[0].shape[0]
     block = 512
-    pieces = spans(256, 256, 2 * hidden)
+    pieces = spans(128, 256, 2 * hidden)
 
     def body(*refs):
         feed_kernel(pieces, 96, block, *refs)
@@ -340,6 +349,7 @@
             scale, q_latent, q_rope, cache_latent, cache_rope, new_latent, new_rope, lengths, counts
         )
         got = exchange(o_latent).reshape(chips, -1, o_latent.shape[1])
+        got, gate2, up2, down2 = lax.optimization_barrier((got, gate2, up2, down2))
         part = project(core, got, w_uv, w_uv2, w_o, w_o2)
         hidden_mine = residual_in.astype(F32) + summed(part, rows)
         normed_mine = normalize(hidden_mine, norm_gain)

time: 104 us -> 99.6 us (0.958)
  blocking collectives: 17.5 us -> 34.1 us
  waiting for transfers between devices: 46.4 us -> 31.9 us
  starting transfers between devices: 15.6 us -> 12.1 us
  Pallas kernels: 20 us -> 18.2 us
    all_to_all x1 -> x2, blocking collectives: 17.5 us -> 34.1 us  [exchange(): lax.all_to_all(v, 'dp', 0, 0, axis_index_groups=same_core, tiled=True)]
    all_to_all x3 -> x2, waiting for transfers between devices: 44.7 us -> 31.9 us  [exchange(): lax.all_to_all(v, 'dp', 0, 0, axis_index_groups=same_core, tiled=True)]
    all_to_all x3 -> x2, starting transfers between devices: 14.6 us -> 10.9 us  [exchange(): lax.all_to_all(v, 'dp', 0, 0, axis_index_groups=same_core, tiled=True)]
    ppermute x5, waiting for transfers between devices: 1.7 us -> 0.01 us  [sibling(): return lax.ppermute(w, 'dp', swap)]
    pallas_call x1, Pallas kernels: 7.21 us -> 6.08 us  [attend(): pl.pallas_call(body, out_shape=jax.ShapeDtypeStruct((heads * rows, width)...]
  transfers between devices with their start and end apart: 8 -> 7, of which waited for: 4 -> 2; matrix products, arithmetic and copies ran while one was open for 1% -> 0% of each run, Pallas kernels for 7% -> 6%
where the time goes in v4:
time: 99.6 us; the launch traced here: 99.2 us
  blocking collectives  34.1 us (34%)
  waiting for transfers between devices  31.9 us (32%)
  Pallas kernels  18.2 us (18%)
  starting transfers between devices  12.1 us (12%)
  other arithmetic  1.14 us (1%)
  local copies, waits for them, and re-layouts  1.03 us (1%)
    all_to_all x2, blocking collectives, exchange(): lax.all_to_all(v, 'dp', 0, 0, axis_index_groups=same_core, tiled=True)  34.1 us
    all_to_all x2, waiting for transfers between devices, exchange(): lax.all_to_all(v, 'dp', 0, 0, axis_index_groups=same_core, tiled=True)  31.9 us
    all_to_all x2, starting transfers between devices, exchange(): lax.all_to_all(v, 'dp', 0, 0, axis_index_groups=same_core, tiled=True)  10.9 us
    pallas_call x1, Pallas kernels, feed(): pl.pallas_call(body, out_shape=jax.ShapeDtypeStruct((rows, width), BF16),...  7.25 us
    pallas_call x1, Pallas kernels, attend(): pl.pallas_call(body, out_shape=jax.ShapeDtypeStruct((heads * rows, width)...  6.08 us
    pallas_call x1, Pallas kernels, project(): pl.pallas_call(body, out_shape=jax.ShapeDtypeStruct((rows, cols), BF16),...  4.86 us
  transfers between devices with their start and end apart: 7, of which 2 were waited for; matrix products, arithmetic and copies ran while one was open for 0% of the time, Pallas kernels for 6%

profile of v4, /device:TPU:192, one launch (start us, length us, event | category | flops | bytes accessed | tf_op | source)
XLA Modules:
  0.0 99.2 jit_solution(10759794256532959343)
XLA Ops:
  0.0 0.0 collective-permute-start.4
  0.0 0.5 collective-permute-start
  0.5 0.0 collective-permute-start.1
  0.5 0.5 collective-permute-start.2
  1.7 6.1 %attend.1 = bf16[1024,512]{1,0:T(8,128)(2,1)} custom-call(s32[8]{0:T(128)} %refs_0_.1, s32[1]{0:T(128)S(6)} %copy.16.refs_1_, bf16[8,512]{1,0:T(8,128)(2,1)} %refs_2_.2, bf16[8,64]{1,0:T(8,128)(2,1)} %refs_3_.1, bf16[8,128,512]{2,1,0:T(8,128)(2,1)} %refs_4_.2, bf16[8,64,128]{2,1,0:T(8,128)(2,1)} %refs_5_.2, bf16[8,384,512]{2,1,0:T(8,128)(2,1)} %refs_6_.1, ...), custom_call_target="tpu_custom_call" | custom-call | flops 805306368 | bytes 5767168 | tf_op jit(solution)/shard_map/attend/pallas_call | solution.py:141
  7.8 0.0 copy-start
  7.8 7.2 %all-to-all-start = ((bf16[16,64,512]{2,1,0:T(8,128)(2,1)}), bf16[16,64,512]{2,1,0:T(8,128)(2,1)S(1)}, u32[]{:S(2)}, u32[]{:S(2)}) async-start(bf16[16,64,512]{2,1,0:T(8,128)(2,1)} %bitcast.9), calls=%async_computation | async-start | bytes 2097152 | tf_op jit(solution)/shard_map/all_to_all | solution.py:319
  15.0 0.0 copy-done
  15.0 0.1 collective-permute-start.3
  15.1 17.9 %all-to-all-done.refs_1_ = bf16[16,64,512]{2,1,0:T(8,128)(2,1)S(1)} async-done(((bf16[16,64,512]{2,1,0:T(8,128)(2,1)}), bf16[16,64,512]{2,1,0:T(8,128)(2,1)S(1)}, u32[]{:S(2)}, u32[]{:S(2)}) %all-to-all-start) | async-done | bytes 1048608 | tf_op jit(solution)/shard_map/all_to_all | solution.py:319
  32.9 0.0 copy-start.1
  32.9 0.0 collective-permute-done.refs_3_
  32.9 0.0 collective-permute-done.1.refs_4_
  32.9 0.0 collective-permute-done.2.refs_6_
  33.0 0.0 collective-permute-done.3.refs_3_
  33.0 0.0 collective-permute-done.4.refs_5_
  33.0 1.0 copy-done.1
  33.9 4.9 %project.1 = bf16[128,3584]{1,0:T(8,128)(2,1)} custom-call(s32[1]{0:T(128)} %bitcast.refs_0_, bf16[16,64,512]{2,1,0:T(8,128)(2,1)} %copy-done.1, bf16[4,512,128]{2,1,0:T(8,128)(2,1)S(1)} %copy-done, bf16[4,512,128]{2,1,0:T(8,128)(2,1)S(1)} %collective-permute-done.3.refs_3_, bf16[512,3584]{1,0:T(8,128)(2,1)} %refs_4_.3, ...), custom_call_target="tpu_custom_call" | custom-call | flops 939524096 | bytes 10354688 | tf_op jit(solution)/shard_map/project/pallas_call | solution.py:216
  38.8 0.0 copy-start.2
  38.8 3.8 %all-to-all-start.1 = ((bf16[16,8,3584]{2,1,0:T(8,128)(2,1)}), bf16[16,8,3584]{2,1,0:T(8,128)(2,1)S(1)}, u32[]{:S(2)}, u32[]{:S(2)}) async-start(bf16[16,8,3584]{2,1,0:T(8,128)(2,1)} %bitcast.4), calls=%async_computation.1 | async-start | bytes 1835008 | tf_op jit(solution)/shard_map/all_to_all | solution.py:319
  42.6 0.0 copy-done.3
  42.6 14.1 %all-to-all-done.1 = bf16[16,8,3584]{2,1,0:T(8,128)(2,1)S(1)} async-done(((bf16[16,8,3584]{2,1,0:T(8,128)(2,1)}), bf16[16,8,3584]{2,1,0:T(8,128)(2,1)S(1)}, u32[]{:S(2)}, u32[]{:S(2)}) %all-to-all-start.1) | async-done | bytes 917536 | tf_op jit(solution)/shard_map/all_to_all | solution.py:319
  56.7 0.1 convert_reduce_fusion.1
  56.8 0.0 copy-done.2
  56.8 0.1 multiply_reduce_fusion
  57.0 0.1 multiply_convert_fusion
  57.1 0.1 broadcast_in_dim.2
  57.1 17.5 %all_to_all.35 = bf16[16,8,3584]{2,1,0:T(8,128)(2,1)S(1)} all-to-all(bf16[16,8,3584]{2,1,0:T(8,128)(2,1)S(1)} %broadcast_in_dim.2), channel_id=1, replica_groups={{0,16,32,48,64,80,96,112,128,144,160,176,192,208,224,240},{8,24,40,56,7..., dimensions={0} | all-to-all | bytes 1835008 | tf_op jit(solution)/shard_map/all_to_all | solution.py:319
  74.7 7.2 %feed.1 = bf16[128,3584]{1,0:T(8,128)(2,1)S(1)} custom-call(bf16[128,3584]{1,0:T(8,128)(2,1)S(1)} %bitcast.7, bf16[288,3584]{1,0:T(8,128)(2,1)} %bitcast.11, bf16[288,3584]{1,0:T(8,128)(2,1)} %bitcast.13, bf16[288,3584]{1,0:T(8,128)(2,1)} %collective-permute-done.refs_3_, bf16[288,3584]{1,0:T(8,128)(2,1)} %collective-permute-done.1.refs_4_, ...), custom_call_target="tpu_custom_call" | custom-call | flops 1585446912 | bytes 14221312 | tf_op jit(solution)/shard_map/feed/pallas_call | solution.py:293
  81.9 16.5 %all_to_all.36 = bf16[16,8,3584]{2,1,0:T(8,128)(2,1)S(1)} all-to-all(bf16[16,8,3584]{2,1,0:T(8,128)(2,1)S(1)} %bitcast.8), channel_id=1, replica_groups={{0,16,32,48,64,80,96,112,128,144,160,176,192,208,224,240},{8,24,40,56,7..., dimensions={0} | all-to-all | bytes 1835008 | tf_op jit(solution)/shard_map/all_to_all | solution.py:319
  98.5 0.1 convert_reduce_fusion
  98.6 0.6 add_convert_fusion
  (3 shorter events, 0.0 us)
Async XLA Ops:
  0.0 33.0 %collective-permute-start.4 = (bf16[512,3584]{1,0:T(8,128)(2,1)}, bf16[512,3584]{1,0:T(8,128)(2,1)}, u32[]{:S(2)}, u32[]{:S(2)}) collective-permute-start(bf16[512,3584]{1,0:T(8,128)(2,1)} %refs_4_.3), channel_id=1, source_target_pairs={{0,8},{8,0},{16,24},{24,16},{32,40},{40,32},{48,56},{56,48},{64,72... | collective-permute-start | bytes 11010056 | tf_op jit(solution)/shard_map/ppermute | solution.py:316
  0.0 32.9 %collective-permute-start = (bf16[288,3584]{1,0:T(8,128)(2,1)}, bf16[288,3584]{1,0:T(8,128)(2,1)}, u32[]{:S(2)}, u32[]{:S(2)}) collective-permute-start(bf16[288,3584]{1,0:T(8,128)(2,1)} %bitcast.10), channel_id=1, source_target_pairs={{0,8},{8,0},{16,24},{24,16},{32,40},{40,32},{48,56},{56,48},{64,72... | collective-permute-start | bytes 6193160 | tf_op jit(solution)/shard_map/ppermute | solution.py:316
  0.5 32.4 %collective-permute-start.1 = (bf16[288,3584]{1,0:T(8,128)(2,1)}, bf16[288,3584]{1,0:T(8,128)(2,1)}, u32[]{:S(2)}, u32[]{:S(2)}) collective-permute-start(bf16[288,3584]{1,0:T(8,128)(2,1)} %bitcast.12), channel_id=1, source_target_pairs={{0,8},{8,0},{16,24},{24,16},{32,40},{40,32},{48,56},{56,48},{64,72... | collective-permute-start | bytes 6193160 | tf_op jit(solution)/shard_map/ppermute | solution.py:316
  0.5 32.4 %collective-permute-start.2 = (bf16[288,3584]{1,0:T(8,128)(2,1)}, bf16[288,3584]{1,0:T(8,128)(2,1)}, u32[]{:S(2)}, u32[]{:S(2)}) collective-permute-start(bf16[288,3584]{1,0:T(8,128)(2,1)} %refs_5_.3), channel_id=1, source_target_pairs={{0,8},{8,0},{16,24},{24,16},{32,40},{40,32},{48,56},{56,48},{64,72... | collective-permute-start | bytes 6193160 | tf_op jit(solution)/shard_map/ppermute | solution.py:316
  7.8 7.2 %copy-start = (bf16[4,512,128]{2,1,0:T(8,128)(2,1)S(1)}, bf16[4,512,128]{2,1,0:T(8,128)(2,1)}, u32[]{:S(2)}) copy-start(bf16[4,512,128]{2,1,0:T(8,128)(2,1)} %refs_2_.3) | copy-start | bytes 1572868
  7.8 25.2 %all-to-all-start = ((bf16[16,64,512]{2,1,0:T(8,128)(2,1)}), bf16[16,64,512]{2,1,0:T(8,128)(2,1)S(1)}, u32[]{:S(2)}, u32[]{:S(2)}) async-start(bf16[16,64,512]{2,1,0:T(8,128)(2,1)} %bitcast.9), calls=%async_computation | async-start | bytes 2097152 | tf_op jit(solution)/shard_map/all_to_all | solution.py:319
  15.0 18.0 %collective-permute-start.3 = (bf16[4,512,128]{2,1,0:T(8,128)(2,1)S(1)}, bf16[4,512,128]{2,1,0:T(8,128)(2,1)S(1)}, u32[]{:S(2)}, u32[]{:S(2)}) collective-permute-start(bf16[4,512,128]{2,1,0:T(8,128)(2,1)S(1)} %copy-done), channel_id=1, source_target_pairs={{0,8},{8,0},{16,24},{24,16},{32,40},{40,32},{48,56},{56,48},{64,72... | collective-permute-start | bytes 1572872 | tf_op jit(solution)/shard_map/ppermute | solution.py:316
  32.9 1.0 %copy-start.1 = (bf16[16,64,512]{2,1,0:T(8,128)(2,1)}, bf16[16,64,512]{2,1,0:T(8,128)(2,1)S(1)}, u32[]{:S(2)}) copy-start(bf16[16,64,512]{2,1,0:T(8,128)(2,1)S(1)} %all-to-all-done.refs_1_) | copy-start | bytes 3145732
  33.9 8.7 %copy-start.3 = (bf16[3584]{0:T(1024)(128)(2,1)S(1)}, bf16[3584]{0:T(1024)(128)(2,1)}, u32[]{:S(2)}) copy-start(bf16[3584]{0:T(1024)(128)(2,1)} %param.26) | copy-start | bytes 21508
  38.8 18.0 %copy-start.2 = (bf16[8,3584]{1,0:T(8,128)(2,1)S(1)}, bf16[8,3584]{1,0:T(8,128)(2,1)}, u32[]{:S(2)}) copy-start(bf16[8,3584]{1,0:T(8,128)(2,1)} %param.15) | copy-start | bytes 172036
  38.8 17.9 %all-to-all-start.1 = ((bf16[16,8,3584]{2,1,0:T(8,128)(2,1)}), bf16[16,8,3584]{2,1,0:T(8,128)(2,1)S(1)}, u32[]{:S(2)}, u32[]{:S(2)}) async-start(bf16[16,8,3584]{2,1,0:T(8,128)(2,1)} %bitcast.4), calls=%async_computation.1 | async-start | bytes 1835008 | tf_op jit(solution)/shard_map/all_to_all | solution.py:319

commit v5 on v4

--- a/solution.py
+++ b/solution.py
@@ -10,6 +10,7 @@
 IN_FLIGHT = 12
 ATTEND_GROUPS = ((0, 2), (2, 8))
 ROOMY_BYTES = 52 * 2**20
+PROJECT_BYTES = 50 * 2**20
 HBM = pl.BlockSpec(memory_space=pltpu.HBM)
 VMEM = pl.BlockSpec(memory_space=pltpu.VMEM)
 SMEM = pl.BlockSpec(memory_space=pltpu.SMEM)
@@ -226,7 +227,7 @@
             pltpu.VMEM((rows, cols), BF16),
             pltpu.SemaphoreType.DMA((3 + 3 * (cols // block),)),
         ],
-        compiler_params=pltpu.CompilerParams(vmem_limit_bytes=ROOMY_BYTES),
+        compiler_params=pltpu.CompilerParams(vmem_limit_bytes=PROJECT_BYTES),
         cost_estimate=cost(4 * rows * w_o.size, size),
         name="project",
     )(core, got, w_uv, w_uv2, w_o, w_o2)

time: 99.6 us -> 98.5 us (0.989)
  no operation moved by 1% of the time
where the time goes in v5:
time: 98.5 us; the launch traced here: 98 us
  blocking collectives  34 us (35%)
  waiting for transfers between devices  32 us (32%)
  Pallas kernels  18 us (18%)
  starting transfers between devices  12.1 us (12%)
  other arithmetic  1.14 us (1%)
    all_to_all x2, blocking collectives, exchange(): lax.all_to_all(v, 'dp', 0, 0, axis_index_groups=same_core, tiled=True)  34 us
    all_to_all x2, waiting for transfers between devices, exchange(): lax.all_to_all(v, 'dp', 0, 0, axis_index_groups=same_core, tiled=True)  31.9 us
    all_to_all x2, starting transfers between devices, exchange(): lax.all_to_all(v, 'dp', 0, 0, axis_index_groups=same_core, tiled=True)  11 us
    pallas_call x1, Pallas kernels, feed(): pl.pallas_call(body, out_shape=jax.ShapeDtypeStruct((rows, width), BF16),...  7.24 us
    pallas_call x1, Pallas kernels, attend(): pl.pallas_call(body, out_shape=jax.ShapeDtypeStruct((heads * rows, width)...  6.08 us
    pallas_call x1, Pallas kernels, project(): pl.pallas_call(body, out_shape=jax.ShapeDtypeStruct((rows, cols), BF16),...  4.64 us
  transfers between devices with their start and end apart: 7, of which 2 were waited for; matrix products, arithmetic and copies ran while one was open for 0% of the time, Pallas kernels for 6%

profile of v5, /device:TPU:192, one launch (start us, length us, event | category | flops | bytes accessed | tf_op | source)
XLA Modules:
  0.0 98.0 jit_solution(6488461822121077508)
XLA Ops:
  0.0 0.0 collective-permute-start.4
  0.0 0.5 collective-permute-start
  0.5 0.0 collective-permute-start.1
  0.5 0.5 collective-permute-start.2
  1.7 6.1 %attend.1 = bf16[1024,512]{1,0:T(8,128)(2,1)} custom-call(s32[8]{0:T(128)} %refs_0_.1, s32[1]{0:T(128)S(6)} %copy.16.refs_1_, bf16[8,512]{1,0:T(8,128)(2,1)} %refs_2_.2, bf16[8,64]{1,0:T(8,128)(2,1)} %refs_3_.1, bf16[8,128,512]{2,1,0:T(8,128)(2,1)} %refs_4_.2, bf16[8,64,128]{2,1,0:T(8,128)(2,1)} %refs_5_.2, bf16[8,384,512]{2,1,0:T(8,128)(2,1)} %refs_6_.1, ...), custom_call_target="tpu_custom_call" | custom-call | flops 805306368 | bytes 5767168 | tf_op jit(solution)/shard_map/attend/pallas_call | solution.py:142
  7.8 0.0 copy-start
  7.8 7.2 %all-to-all-start = ((bf16[16,64,512]{2,1,0:T(8,128)(2,1)}), bf16[16,64,512]{2,1,0:T(8,128)(2,1)S(1)}, u32[]{:S(2)}, u32[]{:S(2)}) async-start(bf16[16,64,512]{2,1,0:T(8,128)(2,1)} %bitcast.9), calls=%async_computation | async-start | bytes 2097152 | tf_op jit(solution)/shard_map/all_to_all | solution.py:320
  15.0 0.0 copy-done
  15.0 0.1 collective-permute-start.3
  15.1 17.9 %all-to-all-done.refs_1_ = bf16[16,64,512]{2,1,0:T(8,128)(2,1)S(1)} async-done(((bf16[16,64,512]{2,1,0:T(8,128)(2,1)}), bf16[16,64,512]{2,1,0:T(8,128)(2,1)S(1)}, u32[]{:S(2)}, u32[]{:S(2)}) %all-to-all-start) | async-done | bytes 1048608 | tf_op jit(solution)/shard_map/all_to_all | solution.py:320
  32.9 0.0 collective-permute-done.refs_3_
  32.9 0.0 collective-permute-done.1.refs_4_
  32.9 0.0 collective-permute-done.2.refs_6_
  32.9 0.0 collective-permute-done.3.refs_3_
  33.0 0.0 collective-permute-done.4.refs_5_
  33.0 0.0 copy-start.2
  33.0 4.6 %project.1 = bf16[128,3584]{1,0:T(8,128)(2,1)} custom-call(s32[1]{0:T(128)} %bitcast.refs_0_, bf16[16,64,512]{2,1,0:T(8,128)(2,1)S(1)} %all-to-all-done.refs_1_, bf16[4,512,128]{2,1,0:T(8,128)(2,1)S(1)} %copy-done, bf16[4,512,128]{2,1,0:T(8,128)(2,1)S(1)} %collective-permute-done.3.refs_3_, bf16[512,3584]{1,0:T(8,128)(2,1)} %refs_4_.3, ...), custom_call_target="tpu_custom_call" | custom-call | flops 939524096 | bytes 10354688 | tf_op jit(solution)/shard_map/project/pallas_call | solution.py:217
  37.6 0.0 copy-start.1
  37.6 3.8 %all-to-all-start.1 = ((bf16[16,8,3584]{2,1,0:T(8,128)(2,1)}), bf16[16,8,3584]{2,1,0:T(8,128)(2,1)S(1)}, u32[]{:S(2)}, u32[]{:S(2)}) async-start(bf16[16,8,3584]{2,1,0:T(8,128)(2,1)} %bitcast.4), calls=%async_computation.1 | async-start | bytes 1835008 | tf_op jit(solution)/shard_map/all_to_all | solution.py:320
  41.4 0.0 copy-done.2
  41.4 14.1 %all-to-all-done.1 = bf16[16,8,3584]{2,1,0:T(8,128)(2,1)S(1)} async-done(((bf16[16,8,3584]{2,1,0:T(8,128)(2,1)}), bf16[16,8,3584]{2,1,0:T(8,128)(2,1)S(1)}, u32[]{:S(2)}, u32[]{:S(2)}) %all-to-all-start.1) | async-done | bytes 917536 | tf_op jit(solution)/shard_map/all_to_all | solution.py:320
  55.5 0.1 convert_reduce_fusion.1
  55.6 0.0 copy-done.1
  55.7 0.1 multiply_reduce_fusion
  55.8 0.1 multiply_convert_fusion
  55.9 0.1 broadcast_in_dim.2
  56.0 17.5 %all_to_all.35 = bf16[16,8,3584]{2,1,0:T(8,128)(2,1)S(1)} all-to-all(bf16[16,8,3584]{2,1,0:T(8,128)(2,1)S(1)} %broadcast_in_dim.2), channel_id=1, replica_groups={{0,16,32,48,64,80,96,112,128,144,160,176,192,208,224,240},{8,24,40,56,7..., dimensions={0} | all-to-all | bytes 1835008 | tf_op jit(solution)/shard_map/all_to_all | solution.py:320
  73.5 7.2 %feed.1 = bf16[128,3584]{1,0:T(8,128)(2,1)S(1)} custom-call(bf16[128,3584]{1,0:T(8,128)(2,1)S(1)} %bitcast.7, bf16[288,3584]{1,0:T(8,128)(2,1)} %bitcast.11, bf16[288,3584]{1,0:T(8,128)(2,1)} %bitcast.13, bf16[288,3584]{1,0:T(8,128)(2,1)} %collective-permute-done.refs_3_, bf16[288,3584]{1,0:T(8,128)(2,1)} %collective-permute-done.1.refs_4_, ...), custom_call_target="tpu_custom_call" | custom-call | flops 1585446912 | bytes 14221312 | tf_op jit(solution)/shard_map/feed/pallas_call | solution.py:294
  80.8 16.5 %all_to_all.36 = bf16[16,8,3584]{2,1,0:T(8,128)(2,1)S(1)} all-to-all(bf16[16,8,3584]{2,1,0:T(8,128)(2,1)S(1)} %bitcast.8), channel_id=1, replica_groups={{0,16,32,48,64,80,96,112,128,144,160,176,192,208,224,240},{8,24,40,56,7..., dimensions={0} | all-to-all | bytes 1835008 | tf_op jit(solution)/shard_map/all_to_all | solution.py:320
  97.3 0.1 convert_reduce_fusion
  97.4 0.6 add_convert_fusion
  (2 shorter events, 0.0 us)
Async XLA Ops:
  0.0 33.0 %collective-permute-start.4 = (bf16[512,3584]{1,0:T(8,128)(2,1)}, bf16[512,3584]{1,0:T(8,128)(2,1)}, u32[]{:S(2)}, u32[]{:S(2)}) collective-permute-start(bf16[512,3584]{1,0:T(8,128)(2,1)} %refs_4_.3), channel_id=1, source_target_pairs={{0,8},{8,0},{16,24},{24,16},{32,40},{40,32},{48,56},{56,48},{64,72... | collective-permute-start | bytes 11010056 | tf_op jit(solution)/shard_map/ppermute | solution.py:317
  0.0 32.9 %collective-permute-start = (bf16[288,3584]{1,0:T(8,128)(2,1)}, bf16[288,3584]{1,0:T(8,128)(2,1)}, u32[]{:S(2)}, u32[]{:S(2)}) collective-permute-start(bf16[288,3584]{1,0:T(8,128)(2,1)} %bitcast.10), channel_id=1, source_target_pairs={{0,8},{8,0},{16,24},{24,16},{32,40},{40,32},{48,56},{56,48},{64,72... | collective-permute-start | bytes 6193160 | tf_op jit(solution)/shard_map/ppermute | solution.py:317
  0.5 32.4 %collective-permute-start.1 = (bf16[288,3584]{1,0:T(8,128)(2,1)}, bf16[288,3584]{1,0:T(8,128)(2,1)}, u32[]{:S(2)}, u32[]{:S(2)}) collective-permute-start(bf16[288,3584]{1,0:T(8,128)(2,1)} %bitcast.12), channel_id=1, source_target_pairs={{0,8},{8,0},{16,24},{24,16},{32,40},{40,32},{48,56},{56,48},{64,72... | collective-permute-start | bytes 6193160 | tf_op jit(solution)/shard_map/ppermute | solution.py:317
  0.5 32.4 %collective-permute-start.2 = (bf16[288,3584]{1,0:T(8,128)(2,1)}, bf16[288,3584]{1,0:T(8,128)(2,1)}, u32[]{:S(2)}, u32[]{:S(2)}) collective-permute-start(bf16[288,3584]{1,0:T(8,128)(2,1)} %refs_5_.3), channel_id=1, source_target_pairs={{0,8},{8,0},{16,24},{24,16},{32,40},{40,32},{48,56},{56,48},{64,72... | collective-permute-start | bytes 6193160 | tf_op jit(solution)/shard_map/ppermute | solution.py:317
  7.8 7.2 %copy-start = (bf16[4,512,128]{2,1,0:T(8,128)(2,1)S(1)}, bf16[4,512,128]{2,1,0:T(8,128)(2,1)}, u32[]{:S(2)}) copy-start(bf16[4,512,128]{2,1,0:T(8,128)(2,1)} %refs_2_.3) | copy-start | bytes 1572868
  7.8 25.2 %all-to-all-start = ((bf16[16,64,512]{2,1,0:T(8,128)(2,1)}), bf16[16,64,512]{2,1,0:T(8,128)(2,1)S(1)}, u32[]{:S(2)}, u32[]{:S(2)}) async-start(bf16[16,64,512]{2,1,0:T(8,128)(2,1)} %bitcast.9), calls=%async_computation | async-start | bytes 2097152 | tf_op jit(solution)/shard_map/all_to_all | solution.py:320
  15.0 18.0 %collective-permute-start.3 = (bf16[4,512,128]{2,1,0:T(8,128)(2,1)S(1)}, bf16[4,512,128]{2,1,0:T(8,128)(2,1)S(1)}, u32[]{:S(2)}, u32[]{:S(2)}) collective-permute-start(bf16[4,512,128]{2,1,0:T(8,128)(2,1)S(1)} %copy-done), channel_id=1, source_target_pairs={{0,8},{8,0},{16,24},{24,16},{32,40},{40,32},{48,56},{56,48},{64,72... | collective-permute-start | bytes 1572872 | tf_op jit(solution)/shard_map/ppermute | solution.py:317
  33.0 8.5 %copy-start.2 = (bf16[3584]{0:T(1024)(128)(2,1)S(1)}, bf16[3584]{0:T(1024)(128)(2,1)}, u32[]{:S(2)}) copy-start(bf16[3584]{0:T(1024)(128)(2,1)} %param.26) | copy-start | bytes 21508
  37.6 18.0 %copy-start.1 = (bf16[8,3584]{1,0:T(8,128)(2,1)S(1)}, bf16[8,3584]{1,0:T(8,128)(2,1)}, u32[]{:S(2)}) copy-start(bf16[8,3584]{1,0:T(8,128)(2,1)} %param.15) | copy-start | bytes 172036
  37.6 17.9 %all-to-all-start.1 = ((bf16[16,8,3584]{2,1,0:T(8,128)(2,1)}), bf16[16,8,3584]{2,1,0:T(8,128)(2,1)S(1)}, u32[]{:S(2)}, u32[]{:S(2)}) async-start(bf16[16,8,3584]{2,1,0:T(8,128)(2,1)} %bitcast.4), calls=%async_computation.1 | async-start | bytes 1835008 | tf_op jit(solution)/shard_map/all_to_all | solution.py:320

commit v6 on v5

--- a/solution.py
+++ b/solution.py
@@ -284,7 +284,7 @@
 def feed(x, *weights):
     rows, width = x.shape
     hidden = weights[0].shape[0]
-    block = 512
+    block = width // 2
     pieces = spans(128, 256, 2 * hidden)
 
     def body(*refs):

time: 98.5 us -> 97.7 us (level)
  no operation moved by 1% of the time
where the time goes in v6:
time: 97.7 us; the launch traced here: 97.3 us
  blocking collectives  34 us (35%)
  waiting for transfers between devices  32 us (33%)
  Pallas kernels  17.2 us (18%)
  starting transfers between devices  12.1 us (12%)
  other arithmetic  1.14 us (1%)
    all_to_all x2, blocking collectives, exchange(): lax.all_to_all(v, 'dp', 0, 0, axis_index_groups=same_core, tiled=True)  34 us
    all_to_all x2, waiting for transfers between devices, exchange(): lax.all_to_all(v, 'dp', 0, 0, axis_index_groups=same_core, tiled=True)  31.9 us
    all_to_all x2, starting transfers between devices, exchange(): lax.all_to_all(v, 'dp', 0, 0, axis_index_groups=same_core, tiled=True)  11 us
    pallas_call x1, Pallas kernels, feed(): pl.pallas_call(body, out_shape=jax.ShapeDtypeStruct((rows, width), BF16),...  6.51 us
    pallas_call x1, Pallas kernels, attend(): pl.pallas_call(body, out_shape=jax.ShapeDtypeStruct((heads * rows, width)...  6.08 us
    pallas_call x1, Pallas kernels, project(): pl.pallas_call(body, out_shape=jax.ShapeDtypeStruct((rows, cols), BF16),...  4.64 us
  transfers between devices with their start and end apart: 7, of which 2 were waited for; matrix products, arithmetic and copies ran while one was open for 0% of the time, Pallas kernels for 6%

profile of v6, /device:TPU:192, one launch (start us, length us, event | category | flops | bytes accessed | tf_op | source)
XLA Modules:
  0.0 97.3 jit_solution(12272204836966511260)
XLA Ops:
  0.0 0.0 collective-permute-start.4
  0.0 0.5 collective-permute-start
  0.5 0.0 collective-permute-start.1
  0.5 0.5 collective-permute-start.2
  1.7 6.1 %attend.1 = bf16[1024,512]{1,0:T(8,128)(2,1)} custom-call(s32[8]{0:T(128)} %refs_0_.1, s32[1]{0:T(128)S(6)} %copy.16.refs_1_, bf16[8,512]{1,0:T(8,128)(2,1)} %refs_2_.2, bf16[8,64]{1,0:T(8,128)(2,1)} %refs_3_.1, bf16[8,128,512]{2,1,0:T(8,128)(2,1)} %refs_4_.2, bf16[8,64,128]{2,1,0:T(8,128)(2,1)} %refs_5_.2, bf16[8,384,512]{2,1,0:T(8,128)(2,1)} %refs_6_.1, ...), custom_call_target="tpu_custom_call" | custom-call | flops 805306368 | bytes 5767168 | tf_op jit(solution)/shard_map/attend/pallas_call | solution.py:142
  7.8 0.0 copy-start
  7.8 7.2 %all-to-all-start = ((bf16[16,64,512]{2,1,0:T(8,128)(2,1)}), bf16[16,64,512]{2,1,0:T(8,128)(2,1)S(1)}, u32[]{:S(2)}, u32[]{:S(2)}) async-start(bf16[16,64,512]{2,1,0:T(8,128)(2,1)} %bitcast.9), calls=%async_computation | async-start | bytes 2097152 | tf_op jit(solution)/shard_map/all_to_all | solution.py:320
  15.0 0.0 copy-done
  15.0 0.1 collective-permute-start.3
  15.1 17.9 %all-to-all-done.refs_1_ = bf16[16,64,512]{2,1,0:T(8,128)(2,1)S(1)} async-done(((bf16[16,64,512]{2,1,0:T(8,128)(2,1)}), bf16[16,64,512]{2,1,0:T(8,128)(2,1)S(1)}, u32[]{:S(2)}, u32[]{:S(2)}) %all-to-all-start) | async-done | bytes 1048608 | tf_op jit(solution)/shard_map/all_to_all | solution.py:320
  32.9 0.0 collective-permute-done.refs_3_
  32.9 0.0 collective-permute-done.1.refs_4_
  32.9 0.0 collective-permute-done.2.refs_6_
  32.9 0.0 collective-permute-done.3.refs_3_
  33.0 0.0 collective-permute-done.4.refs_5_
  33.0 0.0 copy-start.2
  33.0 4.6 %project.1 = bf16[128,3584]{1,0:T(8,128)(2,1)} custom-call(s32[1]{0:T(128)} %bitcast.refs_0_, bf16[16,64,512]{2,1,0:T(8,128)(2,1)S(1)} %all-to-all-done.refs_1_, bf16[4,512,128]{2,1,0:T(8,128)(2,1)S(1)} %copy-done, bf16[4,512,128]{2,1,0:T(8,128)(2,1)S(1)} %collective-permute-done.3.refs_3_, bf16[512,3584]{1,0:T(8,128)(2,1)} %refs_4_.3, ...), custom_call_target="tpu_custom_call" | custom-call | flops 939524096 | bytes 10354688 | tf_op jit(solution)/shard_map/project/pallas_call | solution.py:217
  37.6 0.0 copy-start.1
  37.6 3.8 %all-to-all-start.1 = ((bf16[16,8,3584]{2,1,0:T(8,128)(2,1)}), bf16[16,8,3584]{2,1,0:T(8,128)(2,1)S(1)}, u32[]{:S(2)}, u32[]{:S(2)}) async-start(bf16[16,8,3584]{2,1,0:T(8,128)(2,1)} %bitcast.4), calls=%async_computation.1 | async-start | bytes 1835008 | tf_op jit(solution)/shard_map/all_to_all | solution.py:320
  41.4 0.0 copy-done.2
  41.4 14.1 %all-to-all-done.1 = bf16[16,8,3584]{2,1,0:T(8,128)(2,1)S(1)} async-done(((bf16[16,8,3584]{2,1,0:T(8,128)(2,1)}), bf16[16,8,3584]{2,1,0:T(8,128)(2,1)S(1)}, u32[]{:S(2)}, u32[]{:S(2)}) %all-to-all-start.1) | async-done | bytes 917536 | tf_op jit(solution)/shard_map/all_to_all | solution.py:320
  55.5 0.1 convert_reduce_fusion.1
  55.6 0.0 copy-done.1
  55.7 0.1 multiply_reduce_fusion
  55.8 0.1 multiply_convert_fusion
  55.9 0.1 broadcast_in_dim.2
  56.0 17.5 %all_to_all.35 = bf16[16,8,3584]{2,1,0:T(8,128)(2,1)S(1)} all-to-all(bf16[16,8,3584]{2,1,0:T(8,128)(2,1)S(1)} %broadcast_in_dim.2), channel_id=1, replica_groups={{0,16,32,48,64,80,96,112,128,144,160,176,192,208,224,240},{8,24,40,56,7..., dimensions={0} | all-to-all | bytes 1835008 | tf_op jit(solution)/shard_map/all_to_all | solution.py:320
  73.5 6.5 %feed.1 = bf16[128,3584]{1,0:T(8,128)(2,1)S(1)} custom-call(bf16[128,3584]{1,0:T(8,128)(2,1)S(1)} %bitcast.7, bf16[288,3584]{1,0:T(8,128)(2,1)} %bitcast.11, bf16[288,3584]{1,0:T(8,128)(2,1)} %bitcast.13, bf16[288,3584]{1,0:T(8,128)(2,1)} %collective-permute-done.refs_3_, bf16[288,3584]{1,0:T(8,128)(2,1)} %collective-permute-done.1.refs_4_, ...), custom_call_target="tpu_custom_call" | custom-call | flops 1585446912 | bytes 14221312 | tf_op jit(solution)/shard_map/feed/pallas_call | solution.py:294
  80.0 16.5 %all_to_all.36 = bf16[16,8,3584]{2,1,0:T(8,128)(2,1)S(1)} all-to-all(bf16[16,8,3584]{2,1,0:T(8,128)(2,1)S(1)} %bitcast.8), channel_id=1, replica_groups={{0,16,32,48,64,80,96,112,128,144,160,176,192,208,224,240},{8,24,40,56,7..., dimensions={0} | all-to-all | bytes 1835008 | tf_op jit(solution)/shard_map/all_to_all | solution.py:320
  96.5 0.1 convert_reduce_fusion
  96.7 0.6 add_convert_fusion
  (2 shorter events, 0.0 us)
Async XLA Ops:
  0.0 33.0 %collective-permute-start.4 = (bf16[512,3584]{1,0:T(8,128)(2,1)}, bf16[512,3584]{1,0:T(8,128)(2,1)}, u32[]{:S(2)}, u32[]{:S(2)}) collective-permute-start(bf16[512,3584]{1,0:T(8,128)(2,1)} %refs_4_.3), channel_id=1, source_target_pairs={{0,8},{8,0},{16,24},{24,16},{32,40},{40,32},{48,56},{56,48},{64,72... | collective-permute-start | bytes 11010056 | tf_op jit(solution)/shard_map/ppermute | solution.py:317
  0.0 32.9 %collective-permute-start = (bf16[288,3584]{1,0:T(8,128)(2,1)}, bf16[288,3584]{1,0:T(8,128)(2,1)}, u32[]{:S(2)}, u32[]{:S(2)}) collective-permute-start(bf16[288,3584]{1,0:T(8,128)(2,1)} %bitcast.10), channel_id=1, source_target_pairs={{0,8},{8,0},{16,24},{24,16},{32,40},{40,32},{48,56},{56,48},{64,72... | collective-permute-start | bytes 6193160 | tf_op jit(solution)/shard_map/ppermute | solution.py:317
  0.5 32.4 %collective-permute-start.1 = (bf16[288,3584]{1,0:T(8,128)(2,1)}, bf16[288,3584]{1,0:T(8,128)(2,1)}, u32[]{:S(2)}, u32[]{:S(2)}) collective-permute-start(bf16[288,3584]{1,0:T(8,128)(2,1)} %bitcast.12), channel_id=1, source_target_pairs={{0,8},{8,0},{16,24},{24,16},{32,40},{40,32},{48,56},{56,48},{64,72... | collective-permute-start | bytes 6193160 | tf_op jit(solution)/shard_map/ppermute | solution.py:317
  0.5 32.4 %collective-permute-start.2 = (bf16[288,3584]{1,0:T(8,128)(2,1)}, bf16[288,3584]{1,0:T(8,128)(2,1)}, u32[]{:S(2)}, u32[]{:S(2)}) collective-permute-start(bf16[288,3584]{1,0:T(8,128)(2,1)} %refs_5_.3), channel_id=1, source_target_pairs={{0,8},{8,0},{16,24},{24,16},{32,40},{40,32},{48,56},{56,48},{64,72... | collective-permute-start | bytes 6193160 | tf_op jit(solution)/shard_map/ppermute | solution.py:317
  7.8 7.2 %copy-start = (bf16[4,512,128]{2,1,0:T(8,128)(2,1)S(1)}, bf16[4,512,128]{2,1,0:T(8,128)(2,1)}, u32[]{:S(2)}) copy-start(bf16[4,512,128]{2,1,0:T(8,128)(2,1)} %refs_2_.3) | copy-start | bytes 1572868
  7.8 25.2 %all-to-all-start = ((bf16[16,64,512]{2,1,0:T(8,128)(2,1)}), bf16[16,64,512]{2,1,0:T(8,128)(2,1)S(1)}, u32[]{:S(2)}, u32[]{:S(2)}) async-start(bf16[16,64,512]{2,1,0:T(8,128)(2,1)} %bitcast.9), calls=%async_computation | async-start | bytes 2097152 | tf_op jit(solution)/shard_map/all_to_all | solution.py:320
  15.0 18.0 %collective-permute-start.3 = (bf16[4,512,128]{2,1,0:T(8,128)(2,1)S(1)}, bf16[4,512,128]{2,1,0:T(8,128)(2,1)S(1)}, u32[]{:S(2)}, u32[]{:S(2)}) collective-permute-start(bf16[4,512,128]{2,1,0:T(8,128)(2,1)S(1)} %copy-done), channel_id=1, source_target_pairs={{0,8},{8,0},{16,24},{24,16},{32,40},{40,32},{48,56},{56,48},{64,72... | collective-permute-start | bytes 1572872 | tf_op jit(solution)/shard_map/ppermute | solution.py:317
  33.0 8.5 %copy-start.2 = (bf16[3584]{0:T(1024)(128)(2,1)S(1)}, bf16[3584]{0:T(1024)(128)(2,1)}, u32[]{:S(2)}) copy-start(bf16[3584]{0:T(1024)(128)(2,1)} %param.26) | copy-start | bytes 21508
  37.6 18.0 %copy-start.1 = (bf16[8,3584]{1,0:T(8,128)(2,1)S(1)}, bf16[8,3584]{1,0:T(8,128)(2,1)}, u32[]{:S(2)}) copy-start(bf16[8,3584]{1,0:T(8,128)(2,1)} %param.15) | copy-start | bytes 172036
  37.6 17.9 %all-to-all-start.1 = ((bf16[16,8,3584]{2,1,0:T(8,128)(2,1)}), bf16[16,8,3584]{2,1,0:T(8,128)(2,1)S(1)}, u32[]{:S(2)}, u32[]{:S(2)}) async-start(bf16[16,8,3584]{2,1,0:T(8,128)(2,1)} %bitcast.4), calls=%async_computation.1 | async-start | bytes 1835008 | tf_op jit(solution)/shard_map/all_to_all | solution.py:320
